TPU v7x, 512 devices: a whole 4x8x8 slice. The times are simulated.
512 devices in a mesh: shot: 16 (over y_lo, x), space: 32 (over z, y_hi, core).
Axes of the slice: x: 4, y: 8 (y_hi: 2, y_lo: 4; y = y_hi * 4 + y_lo), z: 8, core: 2. Of those that a mesh axis runs over, the one named last changes fastest.
Arguments:
- courant: float32 [512, 256, 128], P('shot', 'space'), may hold values from 0.05 to 0.18
- anchor: int32 [16, 2], P('shot'), may hold values from 0 to 384, as said below
- source: int32 [16, 3], P('shot'), may hold values from 0 to 127, as said below
- wavelet: float32 [16, 3], P('shot'), may hold values from -12 to 12
- receivers: int32 [16, 64, 3], P('shot'), may hold values from 0 to 127, as said below
- observed: float32 [16, 3, 64], P('shot'), may hold values from -3 to 3
- wave_before: float32 [16, 128, 128, 128], P('shot', 'space'), may hold values from -1.8 to 1.8
- wave_now: float32 [16, 128, 128, 128], P('shot', 'space'), may hold values from -1.8 to 1.8
- adjoint_after: float32 [16, 128, 128, 128], P('shot', 'space'), may hold values from -1.8 to 1.8
- adjoint_now: float32 [16, 128, 128, 128], P('shot', 'space'), may hold values from -1.8 to 1.8
Outputs:
- gradient: float32 [512, 256, 128], P('shot', 'space')
Inputs may be any that keep to these rules, and one draw needn't show every extreme that they name: anchor[s] = (ox, oy) with ox at most 384 and oy at most 128; in each column some shot group has 0 and some the column's largest allowed value. `source`: a cell of the aperture: first coordinate below 128, second below 128, third below 128; in each column some shot group has 0 and some the largest value. `receivers`: cells of the aperture: first coordinate below 128, second below 128, third below 128; cells may repeat; in each column some receiver has 0 and some the largest value.
All inputs are finite; a program needn't handle non-finite values.
Results may differ from a plain program's by a relative error of at most 0.00002.
Values sent between devices are 32-bit elements; how exact they have to be, the bound alone decides.
A program may use at most 64 MiB of HBM per device.

v0:
```python
import jax
import jax.numpy as jnp
from jax import lax
from jax.sharding import PartitionSpec as P

STEPS = 3


stencil_coef = (-205.0 / 72.0, 8.0 / 5.0, -1.0 / 5.0, 8.0 / 315.0, -1.0 / 560.0)


def with_halo(cells, sides, width):
    for axis, dim in sides:
        count = lax.axis_size(axis)
        ends = count - 1
        head = lax.slice_in_dim(cells, 0, width, axis=dim)
        tail = lax.slice_in_dim(cells, cells.shape[dim] - width, cells.shape[dim], axis=dim)
        cells = jnp.concatenate(
            [
                lax.ppermute(tail, axis, [(i, (i + 1) % count) for i in range(ends)]),
                cells,
                lax.ppermute(head, axis, [((i + 1) % count, i) for i in range(ends)]),
            ],
            axis=dim,
        )
    return cells


def stencil(padded, extent_x, extent_y, extent_z):

    def offset_view(shift_x, shift_y, shift_z):
        return padded[
            4 + shift_x : 4 + shift_x + extent_x,
            4 + shift_y : 4 + shift_y + extent_y,
            4 + shift_z : 4 + shift_z + extent_z,
        ]

    total = 3.0 * stencil_coef[0] * offset_view(0, 0, 0)
    for reach in range(1, 5):
        beside_all = offset_view(reach, 0, 0) + offset_view(-reach, 0, 0)
        beside_all = beside_all + offset_view(0, reach, 0) + offset_view(0, -reach, 0)
        beside_all = beside_all + offset_view(0, 0, reach) + offset_view(0, 0, -reach)
        total = total + stencil_coef[reach] * beside_all
    return total


def side_pad(extended):
    return jnp.pad(extended, ((0, 0), (4, 4), (4, 4)))


def on_device(
    courant,
    anchor,
    source,
    wavelet,
    receivers,
    observed,
    wave_before,
    wave_now,
    adjoint_after,
    adjoint_now,
):
    block_rows = wave_now.shape[1]
    col_count = wave_now.shape[2]
    depth_count = wave_now.shape[3]
    space_count = lax.axis_size("space")
    start_row = lax.axis_index("space") * block_rows
    corner_x = anchor[0, 0]
    corner_y = anchor[0, 1]
    all_rows = lax.all_gather(courant, "shot", axis=0, tiled=True)
    window = lax.dynamic_slice_in_dim(all_rows, corner_x, block_rows * space_count, 0)
    columns = lax.all_to_all(window, "space", split_axis=0, concat_axis=1, tiled=True)
    speed_window = lax.dynamic_slice_in_dim(columns, corner_y, col_count, 1)
    source_row = source[0, 0] - start_row
    source_inside = (source_row >= 0) & (source_row < block_rows)
    source_clip = jnp.clip(source_row, 0, block_rows - 1)
    receiver_row = receivers[0, :, 0] - start_row
    receiver_inside = (receiver_row >= 0) & (receiver_row < block_rows)
    receiver_flat = (
        jnp.clip(receiver_row, 0, block_rows - 1) * (col_count * depth_count)
        + receivers[0, :, 1] * depth_count
        + receivers[0, :, 2]
    )

    def inject_source(field, amount):
        return field.at[source_clip, source[0, 1], source[0, 2]].add(
            jnp.where(source_inside, amount, 0.0)
        )

    def inject_residual(field, values):
        flat_field = (
            field.reshape(-1).at[receiver_flat].add(jnp.where(receiver_inside, values, 0.0))
        )
        return flat_field.reshape(field.shape)

    previous = wave_before[0]
    current = wave_now[0]
    laplacians = []
    residuals = []
    for step_index in range(STEPS):
        forward_extended = with_halo(current, (("space", 0),), 4)
        laplace_now = stencil(side_pad(forward_extended), block_rows, col_count, depth_count)
        laplacians.append(laplace_now)
        next_field = inject_source(
            2.0 * current - previous + speed_window * laplace_now, wavelet[0, step_index]
        )
        residuals.append(
            jnp.where(receiver_inside, next_field.reshape(-1)[receiver_flat], 0.0)
            - observed[0, step_index]
        )
        previous, current = (current, next_field)
    farther = adjoint_after[0]
    nearer = inject_residual(adjoint_now[0], residuals[STEPS - 1])
    imaging = jnp.zeros((block_rows, col_count, depth_count), jnp.float32)
    following = current
    present = previous
    for step_index in range(STEPS - 1, -1, -1):
        if step_index > 0:
            paired = with_halo(jnp.stack([speed_window * nearer, present]), (("space", 1),), 4)
            adjoint_lap = stencil(side_pad(paired[0]), block_rows, col_count, depth_count)
            laplace_now = stencil(side_pad(paired[1]), block_rows, col_count, depth_count)
        else:
            extended = with_halo(present, (("space", 0),), 4)
            laplace_now = stencil(side_pad(extended), block_rows, col_count, depth_count)
        imaging = imaging + nearer * laplace_now
        if step_index > 0:
            updated = inject_residual(
                2.0 * nearer - farther + adjoint_lap, residuals[step_index - 1]
            )
            farther, nearer = (nearer, updated)
            earlier = inject_source(
                2.0 * present - following + speed_window * laplace_now, wavelet[0, step_index]
            )
            following, present = (present, earlier)
    spread_rows = jnp.zeros((block_rows, columns.shape[1], depth_count), jnp.float32)
    spread_rows = lax.dynamic_update_slice_in_dim(spread_rows, imaging, corner_y, 1)
    returned = lax.all_to_all(spread_rows, "space", split_axis=1, concat_axis=0, tiled=True)
    placed = lax.dynamic_update_slice_in_dim(
        jnp.zeros(all_rows.shape, jnp.float32), returned, corner_x, 0
    )
    return lax.psum_scatter(placed, "shot", scatter_dimension=0, tiled=True)


def solution(mesh):
    return jax.shard_map(
        on_device,
        mesh=mesh,
        in_specs=(
            P("shot", "space", None),
            P("shot", None),
            P("shot", None),
            P("shot", None),
            P("shot", None, None),
            P("shot", None, None),
            P("shot", "space", None, None),
            P("shot", "space", None, None),
            P("shot", "space", None, None),
            P("shot", "space", None, None),
        ),
        out_specs=P("shot", "space", None),
        check_vma=False,
    )
```

profile of v0, /device:TPU:64, one launch (start us, length us, event | category | flops | bytes accessed | tf_op | source)
XLA Modules:
  0.0 410.5 jit_solution(3708138599731003318)
XLA Ops:
  6.6 0.7 all-gather.2.cloned.1.call-update
  7.3 1.3 fusion.227
  10.5 89.0 %all-gather.2.cloned.1.call-done = f32[512,8,128]{2,1,0:T(8,128)} async-done(((f32[32,8,128]{2,1,0:T(8,128)}), f32[512,8,128]{2,1,0:T(8,128)}) %all-gather.2.cloned.1.call-update) | async-done | bytes 2097168 | tf_op jit(solution)/shard_map/all_gather | solution.py:70
  99.5 1.9 constant_dynamic-slice_fusion
  101.4 11.5 %all-to-all-start = ((f32[128,8,128]{2,1,0:T(8,128)}), f32[128,8,128]{2,1,0:T(8,128)S(1)}, u32[]{:S(2)}, u32[]{:S(2)}) async-start(f32[128,8,128]{2,1,0:T(8,128)} %constant_dynamic-slice_fusion), calls=%async_computation | async-start | bytes 1048576 | tf_op jit(solution)/shard_map/all_to_all | solution.py:72
  113.0 2.1 collective-permute-start.1
  115.1 8.3 %collective-permute-start = (f32[4,128,128]{2,1,0:T(8,128)S(1)}, f32[4,128,128]{2,1,0:T(8,128)S(1)}, u32[]{:S(2)}, u32[]{:S(2)}) collective-permute-start(f32[4,128,128]{2,1,0:T(8,128)S(1)} %bitcast.190), channel_id=1, source_target_pairs={{1,0},{2,1},{3,2},{4,3},{5,4},{6,5},{7,6},{8,7},{9,8},{10,9},{11,1... | collective-permute-start | bytes 786440 | tf_op jit(solution)/shard_map/ppermute | solution.py:22
  123.4 0.7 fusion.226
  130.4 0.7 fusion.225
  131.6 0.8 and_reduce_fusion
  133.6 2.4 fusion.80
  138.4 4.0 collective-permute-start.3
  142.4 6.6 %collective-permute-start.2 = (f32[4,128,128]{2,1,0:T(8,128)S(1)}, f32[4,128,128]{2,1,0:T(8,128)S(1)}, u32[]{:S(2)}, u32[]{:S(2)}) collective-permute-start(f32[4,128,128]{2,1,0:T(8,128)S(1)} %scatter-add.36), channel_id=1, source_target_pairs={{1,0},{2,1},{3,2},{4,3},{5,4},{6,5},{7,6},{8,7},{9,8},{10,9},{11,1... | collective-permute-start | bytes 786440 | tf_op jit(solution)/shard_map/ppermute | solution.py:22
  150.3 3.2 collective-permute-done.3
  154.0 1.1 fusion.58
  157.6 6.9 %collective-permute-start.5 = (f32[4,128,128]{2,1,0:T(8,128)S(1)}, f32[4,128,128]{2,1,0:T(8,128)S(1)}, u32[]{:S(2)}, u32[]{:S(2)}) collective-permute-start(f32[4,128,128]{2,1,0:T(8,128)S(1)} %scatter-add.39), channel_id=1, source_target_pairs={{0,1},{1,2},{2,3},{3,4},{4,5},{5,6},{6,7},{7,8},{8,9},{9,10},{10,1... | collective-permute-start | bytes 786440 | tf_op jit(solution)/shard_map/ppermute | solution.py:20
  164.5 3.4 collective-permute-start.4
  168.0 0.8 gather_fusion.2
  168.8 0.8 gather_fusion.1
  170.1 1.8 collective-permute-done.4
  172.4 1.1 fusion.36
  176.0 0.8 gather_fusion
  176.8 1.0 scatter_fusion
  177.9 6.2 %collective-permute-start.7 = (f32[2,4,128,128]{3,2,1,0:T(8,128)S(1)}, f32[2,4,128,128]{3,2,1,0:T(8,128)S(1)}, u32[]{:S(2)}, u32[]{:S(2)}) collective-permute-start(f32[2,4,128,128]{3,2,1,0:T(8,128)S(1)} %pad_maximum_fusion.4), channel_id=1, source_target_pairs={{0,1},{1,2},{2,3},{3,4},{4,5},{5,6},{6,7},{7,8},{8,9},{9,10},{10,1... | collective-permute-start | bytes 1572872 | tf_op jit(solution)/shard_map/ppermute | solution.py:20
  184.2 4.3 %collective-permute-start.6 = (f32[2,4,128,128]{3,2,1,0:T(8,128)S(1)}, f32[2,4,128,128]{3,2,1,0:T(8,128)S(1)}, u32[]{:S(2)}, u32[]{:S(2)}) collective-permute-start(f32[2,4,128,128]{3,2,1,0:T(8,128)S(1)} %pad_maximum_fusion.4), channel_id=1, source_target_pairs={{1,0},{2,1},{3,2},{4,3},{5,4},{6,5},{7,6},{8,7},{9,8},{10,9},{11,1... | collective-permute-start | bytes 1572872 | tf_op jit(solution)/shard_map/ppermute | solution.py:22
  188.5 4.9 %collective-permute-done.7 = f32[2,4,128,128]{3,2,1,0:T(8,128)S(1)} collective-permute-done((f32[2,4,128,128]{3,2,1,0:T(8,128)S(1)}, f32[2,4,128,128]{3,2,1,0:T(8,128)S(1)}, u32[]{:S(2)}, u32[]{:S(2)}) %collective-permute-start.7) | collective-permute-done | bytes 524320 | tf_op jit(solution)/shard_map/ppermute | solution.py:20
  193.4 6.0 %collective-permute-done.6 = f32[2,4,128,128]{3,2,1,0:T(8,128)S(1)} collective-permute-done((f32[2,4,128,128]{3,2,1,0:T(8,128)S(1)}, f32[2,4,128,128]{3,2,1,0:T(8,128)S(1)}, u32[]{:S(2)}, u32[]{:S(2)}) %collective-permute-start.6) | collective-permute-done | bytes 524320 | tf_op jit(solution)/shard_map/ppermute | solution.py:22
  199.6 1.0 slice_bitcast_fusion.2
  200.8 0.7 copy-done.11
  202.2 1.0 scatter_fusion.1
  203.2 5.7 %multiply_add_fusion.1 = (f32[4,128,128]{2,1,0:T(8,128)S(1)}, f32[4,128,128]{2,1,0:T(8,128)}, f32[1,4,128,128]{3,2,1,0:T(8,128)}) fusion(f32[4,128,128]{2,1,0:T(8,128)S(1)} %scatter-add.48, f32[4,128,128]{2,1,0:T(8,128)S(1)} %scatter-add.39, f32[4,256,128]{2,1,0:T(8,128)S(1)} %bitcast.170, s32[]{:T(128)S(6)} %select_n.75, ...), kind=kLoop, calls=%fused_computation.405 | loop fusion | flops 2228224 | bytes 4718596 | tf_op jit(solution)/shard_map/add | solution.py:132
  211.5 1.0 pad_maximum_fusion.5
  212.5 5.6 %collective-permute-start.9 = (f32[2,4,128,128]{3,2,1,0:T(8,128)S(1)}, f32[2,4,128,128]{3,2,1,0:T(8,128)S(1)}, u32[]{:S(2)}, u32[]{:S(2)}) collective-permute-start(f32[2,4,128,128]{3,2,1,0:T(8,128)S(1)} %pad_maximum_fusion.5), channel_id=1, source_target_pairs={{0,1},{1,2},{2,3},{3,4},{4,5},{5,6},{6,7},{7,8},{8,9},{9,10},{10,1... | collective-permute-start | bytes 1572872 | tf_op jit(solution)/shard_map/ppermute | solution.py:20
  218.1 5.1 %collective-permute-start.8 = (f32[2,4,128,128]{3,2,1,0:T(8,128)S(1)}, f32[2,4,128,128]{3,2,1,0:T(8,128)S(1)}, u32[]{:S(2)}, u32[]{:S(2)}) collective-permute-start(f32[2,4,128,128]{3,2,1,0:T(8,128)S(1)} %pad_maximum_fusion.5), channel_id=1, source_target_pairs={{1,0},{2,1},{3,2},{4,3},{5,4},{6,5},{7,6},{8,7},{9,8},{10,9},{11,1... | collective-permute-start | bytes 1572872 | tf_op jit(solution)/shard_map/ppermute | solution.py:22
  223.2 4.8 %collective-permute-done.9 = f32[2,4,128,128]{3,2,1,0:T(8,128)S(1)} collective-permute-done((f32[2,4,128,128]{3,2,1,0:T(8,128)S(1)}, f32[2,4,128,128]{3,2,1,0:T(8,128)S(1)}, u32[]{:S(2)}, u32[]{:S(2)}) %collective-permute-start.9) | collective-permute-done | bytes 524320 | tf_op jit(solution)/shard_map/ppermute | solution.py:20
  228.0 3.1 collective-permute-done.8
  231.1 1.2 pad_maximum_fusion.1
  232.3 1.0 slice_bitcast_fusion.1
  233.5 1.3 multiply_add_fusion
  237.7 6.9 %collective-permute-start.11 = (f32[4,128,128]{2,1,0:T(8,128)S(1)}, f32[4,128,128]{2,1,0:T(8,128)}, u32[]{:S(2)}, u32[]{:S(2)}) collective-permute-start(f32[4,128,128]{2,1,0:T(8,128)S(1)} %scatter-add.53), channel_id=1, source_target_pairs={{0,1},{1,2},{2,3},{3,4},{4,5},{5,6},{6,7},{7,8},{8,9},{9,10},{10,1... | collective-permute-start | bytes 786440 | tf_op jit(solution)/shard_map/ppermute | solution.py:20
  244.6 3.7 collective-permute-start.10
  248.4 5.1 %fusion.173 = f32[4,128,128]{2,1,0:T(8,128)S(1)} fusion(f32[12,128,128]{2,1,0:T(8,128)} %get-tuple-element.70, f32[2,4,128,128]{3,2,1,0:T(8,128)S(1)} %collective-permute-done.9, f32[2,4,128,128]{3,2,1,0:T(8,128)} %copy-done.4, f32[2,8,128,128]{3,2,1,0:T(8,128)} %copy-done.2, f32[2,8,128,128]{3,2,1,0:T(8,128)S(1)} %get-tuple-element.73, ...), kind=kLoop, calls=%fused_computation.301 | loop fusion | flops 2162688 | bytes 3932164 | tf_op jit(solution)/shard_map/add | solution.py:128
  253.5 1.0 scatter_fusion.2
  254.6 1.5 select_maximum_fusion
  256.1 2.4 fusion.14
  258.9 45.0 %all_to_all.36 = f32[4,256,128]{2,0,1:T(4,128)S(1)} all-to-all(f32[4,256,128]{2,0,1:T(4,128)S(1)} %copy_dynamic-update-slice_fusion), channel_id=1, replica_groups=mesh['shot'=16,'space'=32] {'space'}, dimensions={1} | all-to-all | bytes 1048576 | tf_op jit(solution)/shard_map/all_to_all | solution.py:137
  304.2 1.4 copy-done.1
  305.5 98.1 %reduce-scatter.2.cloned.1.call-done = f32[32,8,128]{2,1,0:T(8,128)} async-done(((f32[512,8,128]{2,1,0:T(8,128)}), f32[32,8,128]{2,1,0:T(8,128)}) %reduce-scatter.2.cloned.1.call-update) | async-done | bytes 131088 | tf_op jit(solution)/shard_map/reduce_scatter | solution.py:141
  (71 shorter events, 8.2 us)
Async XLA Ops:
  6.5 125.1 %copy-start.16 = (s32[3]{0:T(128)S(1)}, s32[3]{0:T(128)}, u32[]{:S(2)}) copy-start(s32[3]{0:T(128)} %constant.131.clone.1) | copy-start | bytes 40
  6.5 116.9 %copy-start.12 = (s32[1,3]{1,0:T(1,128)S(1)}, s32[1,3]{1,0:T(1,128)}, u32[]{:S(2)}) copy-start(s32[1,3]{1,0:T(1,128)} %param.22) | copy-start | bytes 40
  6.5 123.9 %copy-start.13 = (f32[1,3]{1,0:T(1,128)S(1)}, f32[1,3]{1,0:T(1,128)}, u32[]{:S(2)}) copy-start(f32[1,3]{1,0:T(1,128)} %param.23) | copy-start | bytes 40
  6.5 106.5 %copy-start.7 = (f32[1,4,128,128]{3,2,1,0:T(8,128)S(1)}, f32[1,4,128,128]{3,2,1,0:T(8,128)}, u32[]{:S(2)}) copy-start(f32[1,4,128,128]{3,2,1,0:T(8,128)} %param.27) | copy-start | bytes 786436
  6.5 93.0 %all-gather.2.cloned.1.call-start = ((), (), s32[]{:S(2)}) async-start(), calls=%async_computation.3 | async-start | bytes 2228224 | tf_op jit(solution)/shard_map/all_gather | solution.py:70
  101.4 31.9 %all-to-all-start = ((f32[128,8,128]{2,1,0:T(8,128)}), f32[128,8,128]{2,1,0:T(8,128)S(1)}, u32[]{:S(2)}, u32[]{:S(2)}) async-start(f32[128,8,128]{2,1,0:T(8,128)} %constant_dynamic-slice_fusion), calls=%async_computation | async-start | bytes 1048576 | tf_op jit(solution)/shard_map/all_to_all | solution.py:72
  113.0 290.7 %reduce-scatter.2.cloned.1.call-start = ((), (), s32[]{:S(2)}) async-start(), calls=%async_computation.4 | async-start | bytes 2228224 | tf_op jit(solution)/shard_map/reduce_scatter | solution.py:141
  113.0 19.4 %collective-permute-start.1 = (f32[4,128,128]{2,1,0:T(8,128)S(1)}, f32[4,128,128]{2,1,0:T(8,128)S(1)}, u32[]{:S(2)}, u32[]{:S(2)}) collective-permute-start(f32[4,128,128]{2,1,0:T(8,128)S(1)} %bitcast.189), channel_id=1, source_target_pairs={{0,1},{1,2},{2,3},{3,4},{4,5},{5,6},{6,7},{7,8},{8,9},{9,10},{10,1... | collective-permute-start | bytes 786440 | tf_op jit(solution)/shard_map/ppermute | solution.py:20
  115.1 17.7 %collective-permute-start = (f32[4,128,128]{2,1,0:T(8,128)S(1)}, f32[4,128,128]{2,1,0:T(8,128)S(1)}, u32[]{:S(2)}, u32[]{:S(2)}) collective-permute-start(f32[4,128,128]{2,1,0:T(8,128)S(1)} %bitcast.190), channel_id=1, source_target_pairs={{1,0},{2,1},{3,2},{4,3},{5,4},{6,5},{7,6},{8,7},{9,8},{10,9},{11,1... | collective-permute-start | bytes 786440 | tf_op jit(solution)/shard_map/ppermute | solution.py:22
  132.8 0.7 copy-start.9
  138.4 15.1 %collective-permute-start.3 = (f32[4,128,128]{2,1,0:T(8,128)S(1)}, f32[4,128,128]{2,1,0:T(8,128)S(1)}, u32[]{:S(2)}, u32[]{:S(2)}) collective-permute-start(f32[4,128,128]{2,1,0:T(8,128)S(1)} %scatter-add.36), channel_id=1, source_target_pairs={{0,1},{1,2},{2,3},{3,4},{4,5},{5,6},{6,7},{7,8},{8,9},{9,10},{10,1... | collective-permute-start | bytes 786440 | tf_op jit(solution)/shard_map/ppermute | solution.py:20
  142.4 11.1 %collective-permute-start.2 = (f32[4,128,128]{2,1,0:T(8,128)S(1)}, f32[4,128,128]{2,1,0:T(8,128)S(1)}, u32[]{:S(2)}, u32[]{:S(2)}) collective-permute-start(f32[4,128,128]{2,1,0:T(8,128)S(1)} %scatter-add.36), channel_id=1, source_target_pairs={{1,0},{2,1},{3,2},{4,3},{5,4},{6,5},{7,6},{8,7},{9,8},{10,9},{11,1... | collective-permute-start | bytes 786440 | tf_op jit(solution)/shard_map/ppermute | solution.py:22
  154.0 14.0 %copy-start.14 = (s32[1,64,3]{1,0,2:T(1,128)S(1)}, s32[1,64,3]{1,0,2:T(1,128)}, u32[]{:S(2)}) copy-start(s32[1,64,3]{1,0,2:T(1,128)} %param.24) | copy-start | bytes 2308
  157.6 12.5 %collective-permute-start.5 = (f32[4,128,128]{2,1,0:T(8,128)S(1)}, f32[4,128,128]{2,1,0:T(8,128)S(1)}, u32[]{:S(2)}, u32[]{:S(2)}) collective-permute-start(f32[4,128,128]{2,1,0:T(8,128)S(1)} %scatter-add.39), channel_id=1, source_target_pairs={{0,1},{1,2},{2,3},{3,4},{4,5},{5,6},{6,7},{7,8},{8,9},{9,10},{10,1... | collective-permute-start | bytes 786440 | tf_op jit(solution)/shard_map/ppermute | solution.py:20
  164.5 7.3 %collective-permute-start.4 = (f32[4,128,128]{2,1,0:T(8,128)S(1)}, f32[4,128,128]{2,1,0:T(8,128)S(1)}, u32[]{:S(2)}, u32[]{:S(2)}) collective-permute-start(f32[4,128,128]{2,1,0:T(8,128)S(1)} %scatter-add.39), channel_id=1, source_target_pairs={{1,0},{2,1},{3,2},{4,3},{5,4},{6,5},{7,6},{8,7},{9,8},{10,9},{11,1... | collective-permute-start | bytes 786440 | tf_op jit(solution)/shard_map/ppermute | solution.py:22
  172.4 4.4 %copy-start.15 = (f32[1,3,64]{2,0,1:T(1,128)S(1)}, f32[1,3,64]{2,0,1:T(1,128)}, u32[]{:S(2)}) copy-start(f32[1,3,64]{2,0,1:T(1,128)} %param.25) | copy-start | bytes 2308
  172.4 4.4 %copy-start = (f32[1,4,128,128]{3,2,1,0:T(8,128)S(1)}, f32[1,4,128,128]{3,2,1,0:T(8,128)}, u32[]{:S(2)}) copy-start(f32[1,4,128,128]{3,2,1,0:T(8,128)} %param.29) | copy-start | bytes 786436
  177.9 15.5 %collective-permute-start.7 = (f32[2,4,128,128]{3,2,1,0:T(8,128)S(1)}, f32[2,4,128,128]{3,2,1,0:T(8,128)S(1)}, u32[]{:S(2)}, u32[]{:S(2)}) collective-permute-start(f32[2,4,128,128]{3,2,1,0:T(8,128)S(1)} %pad_maximum_fusion.4), channel_id=1, source_target_pairs={{0,1},{1,2},{2,3},{3,4},{4,5},{5,6},{6,7},{7,8},{8,9},{9,10},{10,1... | collective-permute-start | bytes 1572872 | tf_op jit(solution)/shard_map/ppermute | solution.py:20
  184.2 15.3 %collective-permute-start.6 = (f32[2,4,128,128]{3,2,1,0:T(8,128)S(1)}, f32[2,4,128,128]{3,2,1,0:T(8,128)S(1)}, u32[]{:S(2)}, u32[]{:S(2)}) collective-permute-start(f32[2,4,128,128]{3,2,1,0:T(8,128)S(1)} %pad_maximum_fusion.4), channel_id=1, source_target_pairs={{1,0},{2,1},{3,2},{4,3},{5,4},{6,5},{7,6},{8,7},{9,8},{10,9},{11,1... | collective-permute-start | bytes 1572872 | tf_op jit(solution)/shard_map/ppermute | solution.py:22
  199.5 1.3 copy-start.5
  200.6 0.9 copy-start.11
  200.8 1.4 copy-start.3
  212.5 15.6 %collective-permute-start.9 = (f32[2,4,128,128]{3,2,1,0:T(8,128)S(1)}, f32[2,4,128,128]{3,2,1,0:T(8,128)S(1)}, u32[]{:S(2)}, u32[]{:S(2)}) collective-permute-start(f32[2,4,128,128]{3,2,1,0:T(8,128)S(1)} %pad_maximum_fusion.5), channel_id=1, source_target_pairs={{0,1},{1,2},{2,3},{3,4},{4,5},{5,6},{6,7},{7,8},{8,9},{9,10},{10,1... | collective-permute-start | bytes 1572872 | tf_op jit(solution)/shard_map/ppermute | solution.py:20
  218.1 13.0 %collective-permute-start.8 = (f32[2,4,128,128]{3,2,1,0:T(8,128)S(1)}, f32[2,4,128,128]{3,2,1,0:T(8,128)S(1)}, u32[]{:S(2)}, u32[]{:S(2)}) collective-permute-start(f32[2,4,128,128]{3,2,1,0:T(8,128)S(1)} %pad_maximum_fusion.5), channel_id=1, source_target_pairs={{1,0},{2,1},{3,2},{4,3},{5,4},{6,5},{7,6},{8,7},{9,8},{10,9},{11,1... | collective-permute-start | bytes 1572872 | tf_op jit(solution)/shard_map/ppermute | solution.py:22
  231.1 2.4 copy-start.4
  232.3 1.0 copy-start.6
  233.5 1.4 copy-start.2
  237.7 16.8 %collective-permute-start.11 = (f32[4,128,128]{2,1,0:T(8,128)S(1)}, f32[4,128,128]{2,1,0:T(8,128)}, u32[]{:S(2)}, u32[]{:S(2)}) collective-permute-start(f32[4,128,128]{2,1,0:T(8,128)S(1)} %scatter-add.53), channel_id=1, source_target_pairs={{0,1},{1,2},{2,3},{3,4},{4,5},{5,6},{6,7},{7,8},{8,9},{9,10},{10,1... | collective-permute-start | bytes 786440 | tf_op jit(solution)/shard_map/ppermute | solution.py:20
  244.6 9.9 %collective-permute-start.10 = (f32[4,128,128]{2,1,0:T(8,128)S(1)}, f32[4,128,128]{2,1,0:T(8,128)}, u32[]{:S(2)}, u32[]{:S(2)}) collective-permute-start(f32[4,128,128]{2,1,0:T(8,128)S(1)} %scatter-add.53), channel_id=1, source_target_pairs={{1,0},{2,1},{3,2},{4,3},{5,4},{6,5},{7,6},{8,7},{9,8},{10,9},{11,1... | collective-permute-start | bytes 786440 | tf_op jit(solution)/shard_map/ppermute | solution.py:22
  253.5 2.6 copy-start.8
  253.5 2.6 copy-start.10
  304.1 1.4 copy-start.1
Sparse Core Ops, SparseCore 0:
  9.5 90.0 all-gather.1
  305.7 97.9 reduce-scatter.1
where the time goes:
time: 411 us; the launch traced here: 410 us
  waiting for transfers between devices  213 us (52%)
  starting transfers between devices  74.8 us (18%)
  blocking collectives  45 us (11%)
  between operations  33.1 us (8%)
  other arithmetic  29.5 us (7%)
  local copies, waits for them, and re-layouts  15.4 us (4%)
    reduce_scatter x1, waiting for transfers between devices, on_device(): return lax.psum_scatter(placed, 'shot', scatter_dimension=0, tiled=True)  98.1 us
    all_gather x1, waiting for transfers between devices, on_device(): all_rows = lax.all_gather(courant, 'shot', axis=0, tiled=True)  89 us
    all_to_all x1, blocking collectives, on_device(): lax.all_to_all(spread_rows, 'space', split_axis=1, concat_axis=0, tiled=T...  45 us
    ppermute x6, starting transfers between devices, with_halo(): lax.ppermute(tail, axis, [(i, (i + 1) % count) for i in range(ends)])  31.7 us
    ppermute x6, starting transfers between devices, with_halo(): lax.ppermute(head, axis, [((i + 1) % count, i) for i in range(ends)])  31.6 us
    ppermute x6, waiting for transfers between devices, with_halo(): lax.ppermute(tail, axis, [(i, (i + 1) % count) for i in range(ends)])  13.5 us
    all_to_all x1, starting transfers between devices, on_device(): lax.all_to_all(window, 'space', split_axis=0, concat_axis=1, tiled=True)  11.5 us
    ppermute x6, waiting for transfers between devices, with_halo(): lax.ppermute(head, axis, [((i + 1) % count, i) for i in range(ends)])  11.3 us
  transfers between devices with their start and end apart: 15, of which 10 were waited for; matrix products, arithmetic and copies ran while one was open for 3% of the time, Pallas kernels for 0%

commit v1 on v0

v1 whole, which is shorter than its diff:
```python
import jax
import jax.numpy as jnp
import numpy as np
from jax import lax
from jax.experimental import pallas as pl
from jax.experimental.pallas import tpu as pltpu
from jax.sharding import PartitionSpec as P

MESH = pl.DeviceIdType.MESH
HIGH = lax.Precision.HIGHEST
COEF = (-205.0 / 72.0, 8.0 / 5.0, -1.0 / 5.0, 8.0 / 315.0, -1.0 / 560.0)
F32 = jnp.float32
I32 = jnp.int32


def depth_band():
    cell = np.arange(128)
    apart = np.abs(cell[:, None] - cell[None, :])
    band = np.where(apart == 0, 3.0 * COEF[0], 0.0)
    for reach in range(1, 5):
        band = np.where(apart == reach, COEF[reach], band)
    return band.astype(np.float32)


def kernel(
    anchor, source, wavelet, band, receivers, observed, courant, wave_before, wave_now,
    adjoint_after, adjoint_now, out,
    gath, picked, rows, rowsend, cols, halfsend, half, twice, speed,
    pad, before, after_now, after, laps, third, adj, spot, images,
    back_half, back_in, back_send, back_rows, back_pick, back_in_x, back_sum, back_in_y,
    anchors, anchor_own,
    local_sem, field_send, field_recv, y_send, y_recv, a_send, a_recv, x_send, x_recv,
    s_send, s_recv, h_send, h_recv, halo_send, halo_recv,
    bh_send, bh_recv, bs_send, bs_recv, bx_send, bx_recv, by_send, by_recv,
):
    shot = lax.axis_index("shot")
    space = lax.axis_index("space")
    yl, x = shot // 4, shot % 4
    z, yh, c = space // 4, (space // 2) % 2, space % 2
    k = 2 * z + c

    def at_k(other):
        return (shot, (other // 2) * 4 + yh * 2 + other % 2)

    def at_x(other):
        return (yl * 4 + other, space)

    def at_y(other):
        return (other * 4 + x, space)

    partner = (shot, z * 4 + (1 - yh) * 2 + c)
    diagonal = (shot, z * 4 + (1 - yh) * 2 + (1 - c))

    def push(src, dst, send, recv, device):
        return pltpu.make_async_remote_copy(
            src_ref=src, dst_ref=dst, send_sem=send, recv_sem=recv,
            device_id=device, device_id_type=MESH,
        )

    def landed(dst, sem):
        pltpu.make_async_copy(dst, dst, sem).wait()

    for n in range(5):
        pad[n, 0:4] = jnp.zeros((4, 80, 128), F32)
        pad[n, 12:16] = jnp.zeros((4, 80, 128), F32)
        pad[n, 4:12, 0:8] = jnp.zeros((8, 8, 128), F32)
        pad[n, 4:12, 72:80] = jnp.zeros((8, 8, 128), F32)
    ox, oy = anchor[0, 0], anchor[0, 1]
    anchor_own[...] = jnp.full((8, 128), ox, I32)
    anchors[x] = jnp.full((8, 128), ox, I32)

    barrier = pltpu.get_barrier_semaphore()
    for d in range(1, 4):
        pl.semaphore_signal(barrier, 1, device_id=at_x((x + d) % 4), device_id_type=MESH)
        pl.semaphore_signal(barrier, 1, device_id=at_y((yl + d) % 4), device_id_type=MESH)
    for d in range(1, 16):
        pl.semaphore_signal(barrier, 1, device_id=at_k((k + d) % 16), device_id_type=MESH)
    pl.semaphore_signal(barrier, 1, device_id=partner, device_id_type=MESH)
    pl.semaphore_signal(barrier, 1, device_id=diagonal, device_id_type=MESH)
    pl.semaphore_wait(barrier, 23)

    def y_copy(d):
        return push(courant, gath.at[yl], y_send.at[d], y_recv.at[d], at_y((yl + d) % 4))

    own_model = pltpu.make_async_copy(courant, gath.at[yl], local_sem.at[0])
    own_model.start()
    for d in (1, 2, 3):
        y_copy(d).start()

    def a_copy(d):
        return push(anchor_own, anchors.at[x], a_send.at[d], a_recv.at[d], at_x((x + d) % 4))

    for d in (1, 2, 3):
        a_copy(d).start()

    def field_parts(n):
        src = (wave_now, wave_before, adjoint_now, adjoint_after)[n]

        def dst(core):
            if n == 0:
                return pad.at[0, pl.ds(4 + 4 * core, 4), pl.ds(8, 64)]
            return (before, after_now, after)[n - 1].at[pl.ds(4 * core, 4)]

        return src, dst

    def field_copy(n, h):
        src, dst = field_parts(n)
        return push(
            src.at[0, :, pl.ds(64 * h, 64), :], dst(c), field_send.at[n, h], field_recv.at[n, c],
            (shot, z * 4 + 2 * h + yh),
        )

    def stays(h):
        return jnp.logical_and(yh == h, c == h)

    def field_start(n):
        src, dst = field_parts(n)
        for h in range(2):

            @pl.when(stays(h))
            def _():
                pltpu.make_async_copy(
                    src.at[0, :, pl.ds(64 * h, 64), :], dst(c), field_recv.at[n, c]
                ).start()

            @pl.when(jnp.logical_not(stays(h)))
            def _():
                field_copy(n, h).start()

    def field_wait(n):
        src, dst = field_parts(n)
        for core in range(2):
            landed(dst(core), field_recv.at[n, core])

    field_start(0)
    field_start(1)

    row_of = receivers[0, :, 0:1] - 8 * k
    col_of = receivers[0, :, 1:2] - 64 * yh
    inside = (row_of >= 0) & (row_of < 8) & (col_of >= 0) & (col_of < 64)
    flat = jnp.where(inside, row_of * 64 + col_of, -1)
    hit = jnp.where(
        lax.broadcasted_iota(I32, (64, 512), 1) == flat, 1.0, 0.0
    ).astype(F32)
    deep = jnp.where(
        lax.broadcasted_iota(I32, (64, 128), 1) == receivers[0, :, 2:3], 1.0, 0.0
    ).astype(F32)
    square = lax.broadcasted_iota(I32, (64, 64), 0) == lax.broadcasted_iota(I32, (64, 64), 1)
    s_row, s_col, s_dep = source[0, 0] - 8 * k, source[0, 1] - 64 * yh, source[0, 2]
    spot[...] = jnp.where(
        (lax.broadcasted_iota(I32, (8, 64, 128), 0) == s_row)
        & (lax.broadcasted_iota(I32, (8, 64, 128), 1) == s_col)
        & (lax.broadcasted_iota(I32, (8, 64, 128), 2) == s_dep),
        1.0, 0.0,
    ).astype(F32)

    def record(field, n):
        lines = jnp.dot(hit, field.reshape(512, 128), precision=HIGH, preferred_element_type=F32)
        got = jnp.sum(lines * deep, axis=1, keepdims=True)
        seen = jnp.sum(
            jnp.where(square, jnp.broadcast_to(observed[0, n : n + 1, :], (64, 64)), 0.0),
            axis=1, keepdims=True,
        )
        return got - seen

    def inject(residual):
        return lax.dot_general(
            hit, deep * residual, (((0,), (0,)), ((), ())),
            precision=HIGH, preferred_element_type=F32,
        ).reshape(8, 64, 128)

    def halo_parts(n):
        up = push(
            pad.at[n, pl.ds(4, 4), pl.ds(8, 64)], pad.at[n, pl.ds(12, 4), pl.ds(8, 64)],
            halo_send.at[n, 0], halo_recv.at[n, 0], at_k((k + 15) % 16),
        )
        down = push(
            pad.at[n, pl.ds(8, 4), pl.ds(8, 64)], pad.at[n, pl.ds(0, 4), pl.ds(8, 64)],
            halo_send.at[n, 1], halo_recv.at[n, 1], at_k((k + 1) % 16),
        )
        side = push(
            pad.at[n, pl.ds(4, 8), pl.ds(pl.multiple_of(64 - 56 * yh, 8), 8)],
            pad.at[n, pl.ds(4, 8), pl.ds(pl.multiple_of(72 * yh, 8), 8)],
            halo_send.at[n, 2], halo_recv.at[n, 2], partner,
        )
        return up, down, side

    def halo_start(n):
        up, down, side = halo_parts(n)

        @pl.when(k > 0)
        def _():
            up.start()

        @pl.when(k < 15)
        def _():
            down.start()

        side.start()

    def halo_wait(n):
        @pl.when(k > 0)
        def _():
            landed(pad.at[n, pl.ds(0, 4), pl.ds(8, 64)], halo_recv.at[n, 1])

        @pl.when(k < 15)
        def _():
            landed(pad.at[n, pl.ds(12, 4), pl.ds(8, 64)], halo_recv.at[n, 0])

        landed(
            pad.at[n, pl.ds(4, 8), pl.ds(pl.multiple_of(72 - 72 * yh, 8), 8)], halo_recv.at[n, 2]
        )

    def halo_done(n):
        up, down, side = halo_parts(n)

        @pl.when(k > 0)
        def _():
            up.wait_send()

        @pl.when(k < 15)
        def _():
            down.wait_send()

        side.wait_send()

    def laplace(n):
        total = jnp.dot(
            pad[n, 4:12, 8:72].reshape(512, 128), band[...],
            precision=HIGH, preferred_element_type=F32,
        ).reshape(8, 64, 128)
        for d in range(1, 5):
            beside = pad[n, 4 - d : 12 - d, 8:72] + pad[n, 4 + d : 12 + d, 8:72]
            beside += pad[n, 4:12, 8 - d : 72 - d] + pad[n, 4:12, 8 + d : 72 + d]
            total += COEF[d] * beside
        return total

    field_wait(0)
    halo_start(0)

    own_model.wait()
    for d in (1, 2, 3):
        landed(gath.at[(yl + 4 - d) % 4], y_recv.at[d])
        landed(anchors.at[(x + 4 - d) % 4], a_recv.at[d])

    residue = 32 * x + lax.broadcasted_iota(I32, (32, 8, 128), 0)

    def super_of(other):
        start = anchors[other]
        return (start >> 7)[None] + jnp.where(residue < (start & 127)[None], 1, 0)

    def x_copy(d):
        return push(
            picked.at[d], rows.at[pl.ds(pl.multiple_of(32 * x, 32), 32)],
            x_send.at[d], x_recv.at[d], at_x((x + d) % 4),
        )

    for d in (2, 1, 3, 0):
        which = super_of((x + d) % 4)
        chosen = gath[0]
        for q in range(1, 4):
            chosen = jnp.where(which == q, gath[q], chosen)
        if d:
            picked[d] = chosen
            x_copy(d).start()
        else:
            rows[pl.ds(pl.multiple_of(32 * x, 32), 32)] = chosen

    halo_wait(0)
    laps[0] = laplace(0)

    for d in (1, 3, 2):
        landed(rows.at[pl.ds(pl.multiple_of(32 * ((x + 4 - d) % 4), 32), 32)], x_recv.at[d])

    first = ox & 127

    def s_copy(d):
        return push(rowsend.at[d], cols.at[k], s_send.at[d], s_recv.at[d], at_k((k + d) % 16))

    def spread(d, carry):
        other = (k + d) % 16
        for r in range(8):
            rowsend[d, r] = rows[(first + 8 * other + r) & 127]
        s_copy(d).start()
        return carry

    lax.fori_loop(1, 16, spread, 0)
    for r in range(8):
        cols[k, r] = rows[(first + 8 * k + r) & 127]

    field_start(2)
    field_start(3)

    def spread_in(d, carry):
        landed(cols.at[(k + 16 - d) % 16], s_recv.at[d])
        return carry

    lax.fori_loop(1, 16, spread_in, 0)

    turn = oy & 63
    lane_col = lax.broadcasted_iota(I32, (8, 8, 128), 1)

    def columns(h, e, core):
        at = (oy >> 6) + h
        place = 32 * e + 16 * yh + 8 * core + lane_col
        low = cols[4 * at + 2 * e + core]
        high = cols[4 * jnp.minimum(at + 1, 3) + 2 * e + core]
        return jnp.where(place < turn, high, low)

    h_copy = push(halfsend, half.at[yh], h_send, h_recv, partner)
    for e in range(2):
        for core in range(2):
            halfsend[e, core] = columns(1 - yh, e, core)
    h_copy.start()
    for e in range(2):
        for core in range(2):
            half[yh, e, core] = columns(yh, e, core)
    landed(half.at[1 - yh], h_recv)
    for e in range(2):
        for b in range(2):
            for core in range(2):
                t = 4 * e + 2 * b + core
                twice[:, 8 * t : 8 * t + 8] = half[b, e, core]
                twice[:, 64 + 8 * t : 72 + 8 * t] = half[b, e, core]
    for r in range(8):
        speed[r] = twice[r, pl.ds(turn, 64)]

    field_wait(1)
    now = pad[0, 4:12, 8:72]
    new = 2.0 * now - before[...] + speed[...] * laps[0] + wavelet[0, 0] * spot[...]
    pad[1, 4:12, 8:72] = new
    halo_start(1)
    residual0 = record(new, 0)
    halo_wait(1)
    lap = laplace(1)
    laps[1] = lap
    new = (
        2.0 * pad[1, 4:12, 8:72] - pad[0, 4:12, 8:72] + speed[...] * lap
        + wavelet[0, 1] * spot[...]
    )
    pad[2, 4:12, 8:72] = new
    halo_start(2)
    residual1 = record(new, 1)
    halo_wait(2)
    lap = laplace(2)
    laps[2] = lap
    new = (
        2.0 * pad[2, 4:12, 8:72] - pad[1, 4:12, 8:72] + speed[...] * lap
        + wavelet[0, 2] * spot[...]
    )
    third[...] = new
    residual2 = record(third[...], 2)

    field_wait(2)
    adj[0] = after_now[...] + inject(residual2)
    pad[3, 4:12, 8:72] = speed[...] * adj[0]
    halo_start(3)
    images[:, 0:64] = adj[0] * laps[2]
    field_wait(3)
    adj[1] = 2.0 * adj[0] - after[...] + inject(residual1)
    halo_wait(3)
    adj[1] = adj[1] + laplace(3)
    pad[4, 4:12, 8:72] = speed[...] * adj[1]
    halo_start(4)
    images[:, 0:64] = images[:, 0:64] + adj[1] * laps[1]
    third[...] = 2.0 * adj[1] - adj[0] + inject(residual0)
    halo_wait(4)
    image = images[:, 0:64] + (third[...] + laplace(4)) * laps[0]
    images[:, 0:64] = image
    images[:, 64:128] = image

    for r in range(8):
        line = images[r, pl.ds(64 - turn, 64)]
        for e in range(2):
            for b in range(2):
                for core in range(2):
                    t = 4 * e + 2 * b + core
                    back_half[b, e, core, r] = line[8 * t : 8 * t + 8]
    bh_copy = push(back_half.at[1 - yh], back_in, bh_send, bh_recv, partner)
    bh_copy.start()
    bh_copy.wait_recv()

    lane_row = lax.broadcasted_iota(I32, (8, 128), 0)

    def owned(other):
        zz, core = other // 2, other % 2
        e, q = zz % 2, zz // 2
        wraps = jnp.where(32 * e + 16 * yh + 8 * core + lane_row < turn, 1, 0)
        mine = (wraps + ((oy >> 6) + yh) == q)[None]
        theirs = (wraps + ((oy >> 6) + 1 - yh) == q)[None]
        return jnp.where(mine, back_half[yh, e, core], 0.0) + jnp.where(
            theirs, back_in[e, core], 0.0
        )

    def bs_copy(d):
        return push(
            back_send.at[d], back_rows.at[pl.ds(pl.multiple_of(8 * k, 8), 8)],
            bs_send.at[d], bs_recv.at[d], at_k((k + d) % 16),
        )

    def give(d, carry):
        back_send[d] = owned((k + d) % 16)
        bs_copy(d).start()
        return carry

    lax.fori_loop(1, 16, give, 0)
    back_rows[pl.ds(pl.multiple_of(8 * k, 8), 8)] = owned(k)

    def given(d, carry):
        landed(
            back_rows.at[pl.ds(pl.multiple_of(8 * ((k + 16 - d) % 16), 8), 8)], bs_recv.at[d]
        )
        return carry

    lax.fori_loop(1, 16, given, 0)

    def bx_copy(d):
        return push(
            back_pick.at[d], back_in_x.at[x], bx_send.at[d], bx_recv.at[d], at_x((x + d) % 4)
        )

    for d in (2, 1, 3, 0):
        other = (x + d) % 4

        def turned(i, carry):
            value = back_rows[(32 * other + i + 128 - first) & 127]
            back_pick[d, i] = value
            return carry

        lax.fori_loop(0, 32, turned, 0)
        if d:
            bx_copy(d).start()
        else:
            back_in_x[x] = back_pick[0]
    for d in (1, 3, 2):
        landed(back_in_x.at[(x + 4 - d) % 4], bx_recv.at[d])

    def by_copy(d):
        return push(
            back_sum.at[d], back_in_y.at[d], by_send.at[d], by_recv.at[d], at_y((yl + d) % 4)
        )

    for d in (2, 1, 3, 0):
        total = jnp.zeros((32, 8, 128), F32)
        for other in range(4):
            total += jnp.where(super_of(other) == (yl + d) % 4, back_in_x[other], 0.0)
        if d:
            back_sum[d] = total
            by_copy(d).start()
        else:
            back_sum[0] = total
    for d in (1, 2, 3):
        landed(back_in_y.at[d], by_recv.at[d])
    out[...] = back_sum[0] + back_in_y[1] + back_in_y[2] + back_in_y[3]

    for d in (1, 2, 3):
        y_copy(d).wait_send()
        a_copy(d).wait_send()
        x_copy(d).wait_send()
        bx_copy(d).wait_send()
        by_copy(d).wait_send()

    def left(d, carry):
        s_copy(d).wait_send()
        bs_copy(d).wait_send()
        return carry

    lax.fori_loop(1, 16, left, 0)
    h_copy.wait_send()
    bh_copy.wait_send()
    for n in range(5):
        halo_done(n)
    for n in range(4):
        for h in range(2):

            @pl.when(jnp.logical_not(stays(h)))
            def _():
                field_copy(n, h).wait_send()


def on_device(
    courant, anchor, source, wavelet, receivers, observed,
    wave_before, wave_now, adjoint_after, adjoint_now,
):
    vmem, smem, anywhere = pltpu.VMEM, pltpu.SMEM, pl.ANY
    dma = pltpu.SemaphoreType.DMA
    return pl.pallas_call(
        kernel,
        out_shape=jax.ShapeDtypeStruct((32, 8, 128), F32),
        in_specs=[pl.BlockSpec(memory_space=smem)] * 3
        + [pl.BlockSpec(memory_space=vmem)] * 3
        + [pl.BlockSpec(memory_space=anywhere)] * 5,
        out_specs=pl.BlockSpec(memory_space=vmem),
        scratch_shapes=[
            vmem((4, 32, 8, 128), F32),
            vmem((4, 32, 8, 128), F32),
            vmem((128, 8, 128), F32),
            vmem((16, 8, 8, 128), F32),
            vmem((16, 8, 8, 128), F32),
            vmem((2, 2, 8, 8, 128), F32),
            vmem((2, 2, 2, 8, 8, 128), F32),
            vmem((8, 128, 128), F32),
            vmem((8, 64, 128), F32),
            vmem((5, 16, 80, 128), F32),
            vmem((8, 64, 128), F32),
            vmem((8, 64, 128), F32),
            vmem((8, 64, 128), F32),
            vmem((3, 8, 64, 128), F32),
            vmem((8, 64, 128), F32),
            vmem((2, 8, 64, 128), F32),
            vmem((8, 64, 128), F32),
            vmem((8, 128, 128), F32),
            vmem((2, 2, 2, 8, 8, 128), F32),
            vmem((2, 2, 8, 8, 128), F32),
            vmem((16, 8, 8, 128), F32),
            vmem((128, 8, 128), F32),
            vmem((4, 32, 8, 128), F32),
            vmem((4, 32, 8, 128), F32),
            vmem((4, 32, 8, 128), F32),
            vmem((4, 32, 8, 128), F32),
            vmem((4, 8, 128), I32),
            vmem((8, 128), I32),
            dma((1,)),
            dma((4, 2)), dma((4, 2)),
            dma((4,)), dma((4,)),
            dma((4,)), dma((4,)),
            dma((4,)), dma((4,)),
            dma((16,)), dma((16,)),
            dma, dma,
            dma((5, 3)), dma((5, 3)),
            dma, dma,
            dma((16,)), dma((16,)),
            dma((4,)), dma((4,)),
            dma((4,)), dma((4,)),
        ],
        compiler_params=pltpu.CompilerParams(
            collective_id=0, has_side_effects=True, vmem_limit_bytes=40 * 1024 * 1024
        ),
    )(
        anchor, source, wavelet, jnp.asarray(depth_band()), receivers, observed, courant,
        wave_before, wave_now, adjoint_after, adjoint_now,
    )


def solution(mesh):
    return jax.shard_map(
        on_device,
        mesh=mesh,
        in_specs=(
            P("shot", "space", None),
            P("shot", None),
            P("shot", None),
            P("shot", None),
            P("shot", None, None),
            P("shot", None, None),
            P("shot", "space", None, None),
            P("shot", "space", None, None),
            P("shot", "space", None, None),
            P("shot", "space", None, None),
        ),
        out_specs=P("shot", "space", None),
        check_vma=False,
    )
```

time: 411 us -> 142 us (0.35)
  the two profiles are of different devices: /device:TPU:64 before, /device:TPU:1 now
where the time goes in v1:
time: 142 us; the launch traced here: 140 us
  Pallas kernels  133 us (94%)
  local copies, waits for them, and re-layouts  7.58 us (5%)
    pallas_call x1, Pallas kernels, on_device(): pl.pallas_call(kernel, out_shape=jax.ShapeDtypeStruct((32, 8, 128), F32),...  133 us
    unnamed x23, local copies, waits for them, and re-layouts  7.58 us

profile of v1, /device:TPU:1, one launch (start us, length us, event | category | flops | bytes accessed | tf_op | source)
XLA Modules:
  0.0 140.3 jit_solution(3032419462808649085)
XLA Ops:
  0.0 0.0 copy-start.9
  0.0 0.7 copy.13.observed
  0.7 0.0 copy-done.9
  0.7 0.0 copy-start.6
  0.7 0.0 copy-start.7
  0.7 0.0 copy-start.8
  0.7 0.1 copy.12.receivers
  0.8 0.5 copy-done.6
  1.4 0.0 copy-done.7
  1.4 0.0 copy-done.8
  1.4 0.0 copy-start
  1.4 0.9 copy-done
  2.3 0.0 copy-start.1
  2.3 0.9 copy-done.1
  3.3 0.0 copy-start.2
  3.3 0.9 copy-done.2
  4.2 0.0 copy-start.3
  4.2 0.9 copy-done.3
  5.2 0.0 copy-start.4
  5.2 0.9 copy-done.4
  6.1 0.0 copy-start.5
  6.1 0.8 copy-done.5
  6.9 132.7 %shard_map.109 = f32[32,8,128]{2,1,0:T(8,128)S(1)} custom-call(s32[1,2]{1,0:T(1,128)S(1)} %copy-done.6, s32[1,3]{1,0:T(1,128)S(1)} %copy-done.7, f32[1,3]{1,0:T(1,128)S(1)} %copy-done.8, f32[128,128]{1,0:T(8,128)S(1)} %copy-done.5, s32[1,64,3]{2,1,0:T(8,128)S(1)} %copy.12.receivers, f32[1,3,64]{2,1,0:T(4,128)S(1)} %copy.13.observed, ...), custom_call_target="tpu_custom_call" | custom-call | tf_op jit(solution)/shard_map/pallas_call | solution.py:487
  139.7 0.7 copy.15
Async XLA Ops:
  0.0 0.7 copy-start.9
  0.7 0.7 copy-start.6
  0.7 0.7 copy-start.7
  0.7 0.7 copy-start.8
  1.4 0.9 copy-start
  2.3 0.9 copy-start.1
  3.3 0.9 copy-start.2
  4.2 0.9 copy-start.3
  5.2 0.9 copy-start.4
  6.1 0.8 copy-start.5

commit v2 on v1

--- a/solution.py
+++ b/solution.py
@@ -1,6 +1,5 @@
 import jax
 import jax.numpy as jnp
-import numpy as np
 from jax import lax
 from jax.experimental import pallas as pl
 from jax.experimental.pallas import tpu as pltpu
@@ -13,22 +12,13 @@
 I32 = jnp.int32
 
 
-def depth_band():
-    cell = np.arange(128)
-    apart = np.abs(cell[:, None] - cell[None, :])
-    band = np.where(apart == 0, 3.0 * COEF[0], 0.0)
-    for reach in range(1, 5):
-        band = np.where(apart == reach, COEF[reach], band)
-    return band.astype(np.float32)
-
-
 def kernel(
-    anchor, source, wavelet, band, receivers, observed, courant, wave_before, wave_now,
+    anchor_in, source_in, wavelet_in, receivers_in, observed_in, courant, wave_before, wave_now,
     adjoint_after, adjoint_now, out,
     gath, picked, rows, rowsend, cols, halfsend, half, twice, speed,
     pad, before, after_now, after, laps, third, adj, spot, images,
     back_half, back_in, back_send, back_rows, back_pick, back_in_x, back_sum, back_in_y,
-    anchors, anchor_own,
+    anchors, anchor_own, anchor, source, wavelet, receivers, observed, band, hits, deeps, seens,
     local_sem, field_send, field_recv, y_send, y_recv, a_send, a_recv, x_send, x_recv,
     s_send, s_recv, h_send, h_recv, halo_send, halo_recv,
     bh_send, bh_recv, bs_send, bs_recv, bx_send, bx_recv, by_send, by_recv,
@@ -60,11 +50,25 @@
     def landed(dst, sem):
         pltpu.make_async_copy(dst, dst, sem).wait()
 
+    small = [
+        pltpu.make_async_copy(src, dst, local_sem.at[1 + n])
+        for n, (src, dst) in enumerate(
+            (
+                (anchor_in, anchor), (source_in, source), (wavelet_in, wavelet),
+                (receivers_in, receivers), (observed_in, observed),
+            )
+        )
+    ]
+    for copy in small:
+        copy.start()
+
     for n in range(5):
         pad[n, 0:4] = jnp.zeros((4, 80, 128), F32)
         pad[n, 12:16] = jnp.zeros((4, 80, 128), F32)
         pad[n, 4:12, 0:8] = jnp.zeros((8, 8, 128), F32)
         pad[n, 4:12, 72:80] = jnp.zeros((8, 8, 128), F32)
+    for copy in small:
+        copy.wait()
     ox, oy = anchor[0, 0], anchor[0, 1]
     anchor_own[...] = jnp.full((8, 128), ox, I32)
     anchors[x] = jnp.full((8, 128), ox, I32)
@@ -132,20 +136,33 @@
         for core in range(2):
             landed(dst(core), field_recv.at[n, core])
 
-    field_start(0)
-    field_start(1)
-
-    row_of = receivers[0, :, 0:1] - 8 * k
-    col_of = receivers[0, :, 1:2] - 64 * yh
+    square = lax.broadcasted_iota(I32, (64, 64), 0) == lax.broadcasted_iota(I32, (64, 64), 1)
+
+    def upright(row):
+        return jnp.sum(
+            jnp.where(square, jnp.broadcast_to(row.astype(F32), (64, 64)), 0.0),
+            axis=1, keepdims=True,
+        )
+
+    row_of = receivers[0] - 8 * k
+    col_of = receivers[1] - 64 * yh
     inside = (row_of >= 0) & (row_of < 8) & (col_of >= 0) & (col_of < 64)
-    flat = jnp.where(inside, row_of * 64 + col_of, -1)
-    hit = jnp.where(
-        lax.broadcasted_iota(I32, (64, 512), 1) == flat, 1.0, 0.0
+    flat = upright(jnp.where(inside, row_of * 64 + col_of, -1))
+    hits[...] = jnp.where(
+        lax.broadcasted_iota(I32, (64, 512), 1).astype(F32) == flat, 1.0, 0.0
     ).astype(F32)
-    deep = jnp.where(
-        lax.broadcasted_iota(I32, (64, 128), 1) == receivers[0, :, 2:3], 1.0, 0.0
+    deeps[...] = jnp.where(
+        lax.broadcasted_iota(I32, (64, 128), 1).astype(F32) == upright(receivers[2]), 1.0, 0.0
     ).astype(F32)
-    square = lax.broadcasted_iota(I32, (64, 64), 0) == lax.broadcasted_iota(I32, (64, 64), 1)
+    for n in range(3):
+        seens[n] = upright(observed[n])
+    apart = jnp.abs(
+        lax.broadcasted_iota(I32, (128, 128), 0) - lax.broadcasted_iota(I32, (128, 128), 1)
+    )
+    line = jnp.where(apart == 0, 3.0 * COEF[0], 0.0)
+    for reach in range(1, 5):
+        line = jnp.where(apart == reach, COEF[reach], line)
+    band[...] = line.astype(F32)
     s_row, s_col, s_dep = source[0, 0] - 8 * k, source[0, 1] - 64 * yh, source[0, 2]
     spot[...] = jnp.where(
         (lax.broadcasted_iota(I32, (8, 64, 128), 0) == s_row)
@@ -155,17 +172,14 @@
     ).astype(F32)
 
     def record(field, n):
-        lines = jnp.dot(hit, field.reshape(512, 128), precision=HIGH, preferred_element_type=F32)
-        got = jnp.sum(lines * deep, axis=1, keepdims=True)
-        seen = jnp.sum(
-            jnp.where(square, jnp.broadcast_to(observed[0, n : n + 1, :], (64, 64)), 0.0),
-            axis=1, keepdims=True,
-        )
-        return got - seen
+        lines = jnp.dot(
+            hits[...], field.reshape(512, 128), precision=HIGH, preferred_element_type=F32
+        )
+        return jnp.sum(lines * deeps[...], axis=1, keepdims=True) - seens[n]
 
     def inject(residual):
         return lax.dot_general(
-            hit, deep * residual, (((0,), (0,)), ((), ())),
+            hits[...], deeps[...] * residual, (((0,), (0,)), ((), ())),
             precision=HIGH, preferred_element_type=F32,
         ).reshape(8, 64, 128)
 
@@ -235,13 +249,13 @@
             total += COEF[d] * beside
         return total
 
-    field_wait(0)
-    halo_start(0)
-
     own_model.wait()
     for d in (1, 2, 3):
         landed(gath.at[(yl + 4 - d) % 4], y_recv.at[d])
         landed(anchors.at[(x + 4 - d) % 4], a_recv.at[d])
+
+    field_start(0)
+    field_start(1)
 
     residue = 32 * x + lax.broadcasted_iota(I32, (32, 8, 128), 0)
 
@@ -266,9 +280,6 @@
         else:
             rows[pl.ds(pl.multiple_of(32 * x, 32), 32)] = chosen
 
-    halo_wait(0)
-    laps[0] = laplace(0)
-
     for d in (1, 3, 2):
         landed(rows.at[pl.ds(pl.multiple_of(32 * ((x + 4 - d) % 4), 32), 32)], x_recv.at[d])
 
@@ -290,6 +301,11 @@
 
     field_start(2)
     field_start(3)
+
+    field_wait(0)
+    halo_start(0)
+    halo_wait(0)
+    laps[0] = laplace(0)
 
     def spread_in(d, carry):
         landed(cols.at[(k + 16 - d) % 16], s_recv.at[d])
@@ -482,14 +498,12 @@
     courant, anchor, source, wavelet, receivers, observed,
     wave_before, wave_now, adjoint_after, adjoint_now,
 ):
-    vmem, smem, anywhere = pltpu.VMEM, pltpu.SMEM, pl.ANY
+    vmem, smem = pltpu.VMEM, pltpu.SMEM
     dma = pltpu.SemaphoreType.DMA
     return pl.pallas_call(
         kernel,
         out_shape=jax.ShapeDtypeStruct((32, 8, 128), F32),
-        in_specs=[pl.BlockSpec(memory_space=smem)] * 3
-        + [pl.BlockSpec(memory_space=vmem)] * 3
-        + [pl.BlockSpec(memory_space=anywhere)] * 5,
+        in_specs=[pl.BlockSpec(memory_space=pltpu.HBM)] * 10,
         out_specs=pl.BlockSpec(memory_space=vmem),
         scratch_shapes=[
             vmem((4, 32, 8, 128), F32),
@@ -520,7 +534,16 @@
             vmem((4, 32, 8, 128), F32),
             vmem((4, 8, 128), I32),
             vmem((8, 128), I32),
-            dma((1,)),
+            smem((1, 2), I32),
+            smem((1, 3), I32),
+            smem((1, 3), F32),
+            vmem((3, 1, 64), I32),
+            vmem((3, 1, 64), F32),
+            vmem((128, 128), F32),
+            vmem((64, 512), F32),
+            vmem((64, 128), F32),
+            vmem((3, 64, 1), F32),
+            dma((6,)),
             dma((4, 2)), dma((4, 2)),
             dma((4,)), dma((4,)),
             dma((4,)), dma((4,)),
@@ -534,10 +557,10 @@
             dma((4,)), dma((4,)),
         ],
         compiler_params=pltpu.CompilerParams(
-            collective_id=0, has_side_effects=True, vmem_limit_bytes=40 * 1024 * 1024
+            collective_id=0, has_side_effects=True, vmem_limit_bytes=60 * 1024 * 1024
         ),
     )(
-        anchor, source, wavelet, jnp.asarray(depth_band()), receivers, observed, courant,
+        anchor, source, wavelet, receivers.transpose(2, 0, 1), observed.transpose(1, 0, 2), courant,
         wave_before, wave_now, adjoint_after, adjoint_now,
     )
 

time: 142 us -> 131 us (0.923)
  local copies, waits for them, and re-layouts: 7.58 us -> 1.57 us
  Pallas kernels: 133 us -> 128 us
    unnamed x23 -> x1, local copies, waits for them, and re-layouts: 7.58 us -> 1.57 us
    pallas_call x1, Pallas kernels: 133 us -> 128 us  [on_device(): pl.pallas_call(kernel, out_shape=jax.ShapeDtypeStruct((32, 8, 128), F32),...]
where the time goes in v2:
time: 131 us; the launch traced here: 130 us
  Pallas kernels  128 us (98%)
  local copies, waits for them, and re-layouts  1.57 us (1%)
    pallas_call x1, Pallas kernels, on_device(): pl.pallas_call(kernel, out_shape=jax.ShapeDtypeStruct((32, 8, 128), F32),...  128 us

profile of v2, /device:TPU:1, one launch (start us, length us, event | category | flops | bytes accessed | tf_op | source)
XLA Modules:
  0.0 129.6 jit_solution(10766586170700670804)
XLA Ops:
  0.0 128.0 %shard_map.100 = f32[32,8,128]{2,1,0:T(8,128)} custom-call(s32[1,2]{1,0:T(1,128)} %anchor_in.1, s32[1,3]{1,0:T(1,128)} %source_in.1, f32[1,3]{1,0:T(1,128)} %wavelet_in.1, s32[3,1,64]{2,1,0:T(1,128)} %bitcast.2, f32[3,1,64]{2,1,0:T(1,128)} %bitcast.3, f32[32,8,128]{2,1,0:T(8,128)} %courant.1, f32[1,4,128,128]{3,2,1,0:T(8,128)} %wave_before.1, ...), custom_call_target="tpu_custom_call" | custom-call | tf_op jit(solution)/shard_map/pallas_call | solution.py:503
  128.0 1.6 %copy.12 = f32[32,8,128]{2,1,0:T(8,128)} copy(f32[32,8,128]{2,1,0:T(8,128)} %shard_map.100) | data formatting | bytes 262144

commit v3 on v2

--- a/solution.py
+++ b/solution.py
@@ -10,19 +10,22 @@
 COEF = (-205.0 / 72.0, 8.0 / 5.0, -1.0 / 5.0, 8.0 / 315.0, -1.0 / 560.0)
 F32 = jnp.float32
 I32 = jnp.int32
+PARTS = 2
+WIDE = 8 // PARTS
 
 
 def kernel(
     anchor_in, source_in, wavelet_in, receivers_in, observed_in, courant, wave_before, wave_now,
     adjoint_after, adjoint_now, out,
-    gath, picked, rows, rowsend, cols, halfsend, half, twice, speed,
+    gath, picked, rows_0, rows_1, rowsend, cols_0, cols_1, halfsend, half, twice, speed,
     pad, before, after_now, after, laps, third, adj, spot, images,
-    back_half, back_in, back_send, back_rows, back_pick, back_in_x, back_sum, back_in_y,
+    back_half, back_in, back_send, back_rows_0, back_rows_1, back_pick, back_in_x, back_sum, back_in_y,
     anchors, anchor_own, anchor, source, wavelet, receivers, observed, band, hits, deeps, seens,
     local_sem, field_send, field_recv, y_send, y_recv, a_send, a_recv, x_send, x_recv,
     s_send, s_recv, h_send, h_recv, halo_send, halo_recv,
     bh_send, bh_recv, bs_send, bs_recv, bx_send, bx_recv, by_send, by_recv,
 ):
+    rows, cols, back_rows = (rows_0, rows_1), (cols_0, cols_1), (back_rows_0, back_rows_1)
     shot = lax.axis_index("shot")
     space = lax.axis_index("space")
     yl, x = shot // 4, shot % 4
@@ -83,19 +86,26 @@
     pl.semaphore_signal(barrier, 1, device_id=diagonal, device_id_type=MESH)
     pl.semaphore_wait(barrier, 23)
 
-    def y_copy(d):
-        return push(courant, gath.at[yl], y_send.at[d], y_recv.at[d], at_y((yl + d) % 4))
+    def part(g):
+        return pl.ds(WIDE * g, WIDE)
+
+    def y_copy(g, d):
+        return push(
+            courant.at[:, part(g), :], gath.at[yl, :, part(g), :],
+            y_send.at[g, d], y_recv.at[g, d], at_y((yl + d) % 4),
+        )
 
     own_model = pltpu.make_async_copy(courant, gath.at[yl], local_sem.at[0])
     own_model.start()
-    for d in (1, 2, 3):
-        y_copy(d).start()
 
     def a_copy(d):
         return push(anchor_own, anchors.at[x], a_send.at[d], a_recv.at[d], at_x((x + d) % 4))
 
     for d in (1, 2, 3):
         a_copy(d).start()
+    for g in range(PARTS):
+        for d in (2, 1, 3):
+            y_copy(g, d).start()
 
     def field_parts(n):
         src = (wave_now, wave_before, adjoint_now, adjoint_after)[n]
@@ -251,87 +261,102 @@
 
     own_model.wait()
     for d in (1, 2, 3):
-        landed(gath.at[(yl + 4 - d) % 4], y_recv.at[d])
         landed(anchors.at[(x + 4 - d) % 4], a_recv.at[d])
 
+    def super_of(other, g):
+        start = anchors[other, part(g), :]
+        residue = 32 * x + lax.broadcasted_iota(I32, (32, WIDE, 128), 0)
+        return (start >> 7)[None] + jnp.where(residue < (start & 127)[None], 1, 0)
+
+    def x_copy(g, d):
+        return push(
+            picked.at[d, :, part(g), :],
+            rows[g].at[pl.ds(pl.multiple_of(32 * x, 32), 32), part(g), :],
+            x_send.at[g, d], x_recv.at[g, d], at_x((x + d) % 4),
+        )
+
+    for g in range(PARTS):
+        for d in (1, 3, 2):
+            landed(gath.at[(yl + 4 - d) % 4, :, part(g), :], y_recv.at[g, d])
+        for d in (2, 1, 3, 0):
+            which = super_of((x + d) % 4, g)
+            chosen = gath[0, :, part(g), :]
+            for q in range(1, 4):
+                chosen = jnp.where(which == q, gath[q, :, part(g), :], chosen)
+            if d:
+                picked[d, :, part(g), :] = chosen
+                x_copy(g, d).start()
+            else:
+                rows[g][pl.ds(pl.multiple_of(32 * x, 32), 32), part(g), :] = chosen
     field_start(0)
     field_start(1)
 
-    residue = 32 * x + lax.broadcasted_iota(I32, (32, 8, 128), 0)
-
-    def super_of(other):
-        start = anchors[other]
-        return (start >> 7)[None] + jnp.where(residue < (start & 127)[None], 1, 0)
-
-    def x_copy(d):
-        return push(
-            picked.at[d], rows.at[pl.ds(pl.multiple_of(32 * x, 32), 32)],
-            x_send.at[d], x_recv.at[d], at_x((x + d) % 4),
-        )
-
-    for d in (2, 1, 3, 0):
-        which = super_of((x + d) % 4)
-        chosen = gath[0]
-        for q in range(1, 4):
-            chosen = jnp.where(which == q, gath[q], chosen)
-        if d:
-            picked[d] = chosen
-            x_copy(d).start()
-        else:
-            rows[pl.ds(pl.multiple_of(32 * x, 32), 32)] = chosen
-
-    for d in (1, 3, 2):
-        landed(rows.at[pl.ds(pl.multiple_of(32 * ((x + 4 - d) % 4), 32), 32)], x_recv.at[d])
-
     first = ox & 127
 
-    def s_copy(d):
-        return push(rowsend.at[d], cols.at[k], s_send.at[d], s_recv.at[d], at_k((k + d) % 16))
-
-    def spread(d, carry):
-        other = (k + d) % 16
+    def s_copy(g, d):
+        return push(
+            rowsend.at[d, :, part(g), :], cols[g].at[k, :, part(g), :],
+            s_send.at[g, d], s_recv.at[g, d], at_k((k + d) % 16),
+        )
+
+    for g in range(PARTS):
+        for d in (1, 3, 2):
+            landed(
+                rows[g].at[pl.ds(pl.multiple_of(32 * ((x + 4 - d) % 4), 32), 32), part(g), :],
+                x_recv.at[g, d],
+            )
+
+        def spread(n, carry):
+            d = (n + 8) % 16
+            other = (k + d) % 16
+            for r in range(8):
+                rowsend[d, r, part(g), :] = rows[g][(first + 8 * other + r) & 127, part(g), :]
+            s_copy(g, d).start()
+            return carry
+
+        lax.fori_loop(0, 8, spread, 0)
+        lax.fori_loop(9, 16, spread, 0)
         for r in range(8):
-            rowsend[d, r] = rows[(first + 8 * other + r) & 127]
-        s_copy(d).start()
-        return carry
-
-    lax.fori_loop(1, 16, spread, 0)
-    for r in range(8):
-        cols[k, r] = rows[(first + 8 * k + r) & 127]
-
+            cols[g][k, r, part(g), :] = rows[g][(first + 8 * k + r) & 127, part(g), :]
+
+    turn = oy & 63
+
+    def columns(h, e, core, g):
+        at = (oy >> 6) + h
+        place = 32 * e + 16 * yh + 8 * core + WIDE * g + lax.broadcasted_iota(I32, (8, WIDE, 128), 1)
+        low = cols[g][4 * at + 2 * e + core, :, part(g), :]
+        high = cols[g][4 * jnp.minimum(at + 1, 3) + 2 * e + core, :, part(g), :]
+        return jnp.where(place < turn, high, low)
+
+    def h_copy(g):
+        return push(
+            halfsend.at[:, :, :, part(g), :], half.at[yh, :, :, :, part(g), :],
+            h_send.at[g], h_recv.at[g], partner,
+        )
+
+    for g in range(PARTS):
+
+        def spread_in(d, carry):
+            landed(cols[g].at[(k + 16 - d) % 16, :, part(g), :], s_recv.at[g, d])
+            return carry
+
+        lax.fori_loop(1, 16, spread_in, 0)
+        for e in range(2):
+            for core in range(2):
+                halfsend[e, core, :, part(g), :] = columns(1 - yh, e, core, g)
+        h_copy(g).start()
+        for e in range(2):
+            for core in range(2):
+                half[yh, e, core, :, part(g), :] = columns(yh, e, core, g)
+        if g == 0:
+            field_wait(0)
+            halo_start(0)
     field_start(2)
     field_start(3)
-
-    field_wait(0)
-    halo_start(0)
     halo_wait(0)
     laps[0] = laplace(0)
-
-    def spread_in(d, carry):
-        landed(cols.at[(k + 16 - d) % 16], s_recv.at[d])
-        return carry
-
-    lax.fori_loop(1, 16, spread_in, 0)
-
-    turn = oy & 63
-    lane_col = lax.broadcasted_iota(I32, (8, 8, 128), 1)
-
-    def columns(h, e, core):
-        at = (oy >> 6) + h
-        place = 32 * e + 16 * yh + 8 * core + lane_col
-        low = cols[4 * at + 2 * e + core]
-        high = cols[4 * jnp.minimum(at + 1, 3) + 2 * e + core]
-        return jnp.where(place < turn, high, low)
-
-    h_copy = push(halfsend, half.at[yh], h_send, h_recv, partner)
-    for e in range(2):
-        for core in range(2):
-            halfsend[e, core] = columns(1 - yh, e, core)
-    h_copy.start()
-    for e in range(2):
-        for core in range(2):
-            half[yh, e, core] = columns(yh, e, core)
-    landed(half.at[1 - yh], h_recv)
+    for g in range(PARTS):
+        landed(half.at[1 - yh, :, :, :, part(g), :], h_recv.at[g])
     for e in range(2):
         for b in range(2):
             for core in range(2):
@@ -392,98 +417,122 @@
                 for core in range(2):
                     t = 4 * e + 2 * b + core
                     back_half[b, e, core, r] = line[8 * t : 8 * t + 8]
-    bh_copy = push(back_half.at[1 - yh], back_in, bh_send, bh_recv, partner)
-    bh_copy.start()
-    bh_copy.wait_recv()
-
-    lane_row = lax.broadcasted_iota(I32, (8, 128), 0)
-
-    def owned(other):
+
+    def bh_copy(g):
+        return push(
+            back_half.at[1 - yh, :, :, :, part(g), :], back_in.at[:, :, :, part(g), :],
+            bh_send.at[g], bh_recv.at[g], partner,
+        )
+
+    for g in range(PARTS):
+        bh_copy(g).start()
+
+    def owned(other, g):
         zz, core = other // 2, other % 2
         e, q = zz % 2, zz // 2
-        wraps = jnp.where(32 * e + 16 * yh + 8 * core + lane_row < turn, 1, 0)
+        place = 32 * e + 16 * yh + 8 * core + WIDE * g + lax.broadcasted_iota(I32, (WIDE, 128), 0)
+        wraps = jnp.where(place < turn, 1, 0)
         mine = (wraps + ((oy >> 6) + yh) == q)[None]
         theirs = (wraps + ((oy >> 6) + 1 - yh) == q)[None]
-        return jnp.where(mine, back_half[yh, e, core], 0.0) + jnp.where(
-            theirs, back_in[e, core], 0.0
-        )
-
-    def bs_copy(d):
-        return push(
-            back_send.at[d], back_rows.at[pl.ds(pl.multiple_of(8 * k, 8), 8)],
-            bs_send.at[d], bs_recv.at[d], at_k((k + d) % 16),
-        )
-
-    def give(d, carry):
-        back_send[d] = owned((k + d) % 16)
-        bs_copy(d).start()
-        return carry
-
-    lax.fori_loop(1, 16, give, 0)
-    back_rows[pl.ds(pl.multiple_of(8 * k, 8), 8)] = owned(k)
-
-    def given(d, carry):
-        landed(
-            back_rows.at[pl.ds(pl.multiple_of(8 * ((k + 16 - d) % 16), 8), 8)], bs_recv.at[d]
-        )
-        return carry
-
-    lax.fori_loop(1, 16, given, 0)
-
-    def bx_copy(d):
-        return push(
-            back_pick.at[d], back_in_x.at[x], bx_send.at[d], bx_recv.at[d], at_x((x + d) % 4)
-        )
-
-    for d in (2, 1, 3, 0):
-        other = (x + d) % 4
-
-        def turned(i, carry):
-            value = back_rows[(32 * other + i + 128 - first) & 127]
-            back_pick[d, i] = value
+        return jnp.where(mine, back_half[yh, e, core, :, part(g), :], 0.0) + jnp.where(
+            theirs, back_in[e, core, :, part(g), :], 0.0
+        )
+
+    def bs_copy(g, d):
+        return push(
+            back_send.at[d, :, part(g), :],
+            back_rows[g].at[pl.ds(pl.multiple_of(8 * k, 8), 8), part(g), :],
+            bs_send.at[g, d], bs_recv.at[g, d], at_k((k + d) % 16),
+        )
+
+    for g in range(PARTS):
+        landed(back_in.at[:, :, :, part(g), :], bh_recv.at[g])
+
+        def give(n, carry):
+            d = (n + 8) % 16
+            back_send[d, :, part(g), :] = owned((k + d) % 16, g)
+            bs_copy(g, d).start()
             return carry
 
-        lax.fori_loop(0, 32, turned, 0)
-        if d:
-            bx_copy(d).start()
-        else:
-            back_in_x[x] = back_pick[0]
-    for d in (1, 3, 2):
-        landed(back_in_x.at[(x + 4 - d) % 4], bx_recv.at[d])
-
-    def by_copy(d):
-        return push(
-            back_sum.at[d], back_in_y.at[d], by_send.at[d], by_recv.at[d], at_y((yl + d) % 4)
-        )
-
-    for d in (2, 1, 3, 0):
-        total = jnp.zeros((32, 8, 128), F32)
-        for other in range(4):
-            total += jnp.where(super_of(other) == (yl + d) % 4, back_in_x[other], 0.0)
-        if d:
-            back_sum[d] = total
-            by_copy(d).start()
-        else:
-            back_sum[0] = total
+        lax.fori_loop(0, 8, give, 0)
+        lax.fori_loop(9, 16, give, 0)
+        back_rows[g][pl.ds(pl.multiple_of(8 * k, 8), 8), part(g), :] = owned(k, g)
+
+    def bx_copy(g, d):
+        return push(
+            back_pick.at[d, :, part(g), :], back_in_x.at[x, :, part(g), :],
+            bx_send.at[g, d], bx_recv.at[g, d], at_x((x + d) % 4),
+        )
+
+    for g in range(PARTS):
+
+        def given(d, carry):
+            landed(
+                back_rows[g].at[
+                    pl.ds(pl.multiple_of(8 * ((k + 16 - d) % 16), 8), 8), part(g), :
+                ],
+                bs_recv.at[g, d],
+            )
+            return carry
+
+        lax.fori_loop(1, 16, given, 0)
+        for d in (2, 1, 3, 0):
+            other = (x + d) % 4
+
+            def turned(n, carry):
+                for r in range(8):
+                    i = 8 * n + r
+                    back_pick[d, i, part(g), :] = back_rows[g][
+                        (32 * other + i + 128 - first) & 127, part(g), :
+                    ]
+                return carry
+
+            lax.fori_loop(0, 4, turned, 0)
+            if d:
+                bx_copy(g, d).start()
+            else:
+                back_in_x[x, :, part(g), :] = back_pick[0, :, part(g), :]
+
+    def by_copy(g, d):
+        return push(
+            back_sum.at[d, :, part(g), :], back_in_y.at[d, :, part(g), :],
+            by_send.at[g, d], by_recv.at[g, d], at_y((yl + d) % 4),
+        )
+
+    for g in range(PARTS):
+        for d in (1, 3, 2):
+            landed(back_in_x.at[(x + 4 - d) % 4, :, part(g), :], bx_recv.at[g, d])
+        for d in (2, 1, 3, 0):
+            total = jnp.zeros((32, WIDE, 128), F32)
+            for other in range(4):
+                total += jnp.where(
+                    super_of(other, g) == (yl + d) % 4, back_in_x[other, :, part(g), :], 0.0
+                )
+            back_sum[d, :, part(g), :] = total
+            if d:
+                by_copy(g, d).start()
+    for g in range(PARTS):
+        for d in (1, 2, 3):
+            landed(back_in_y.at[d, :, part(g), :], by_recv.at[g, d])
+    out[...] = back_sum[0] + back_in_y[1] + back_in_y[2] + back_in_y[3]
+
     for d in (1, 2, 3):
-        landed(back_in_y.at[d], by_recv.at[d])
-    out[...] = back_sum[0] + back_in_y[1] + back_in_y[2] + back_in_y[3]
-
-    for d in (1, 2, 3):
-        y_copy(d).wait_send()
         a_copy(d).wait_send()
-        x_copy(d).wait_send()
-        bx_copy(d).wait_send()
-        by_copy(d).wait_send()
-
-    def left(d, carry):
-        s_copy(d).wait_send()
-        bs_copy(d).wait_send()
-        return carry
-
-    lax.fori_loop(1, 16, left, 0)
-    h_copy.wait_send()
-    bh_copy.wait_send()
+    for g in range(PARTS):
+        for d in (1, 2, 3):
+            y_copy(g, d).wait_send()
+            x_copy(g, d).wait_send()
+            bx_copy(g, d).wait_send()
+            by_copy(g, d).wait_send()
+
+        def left(d, carry):
+            s_copy(g, d).wait_send()
+            bs_copy(g, d).wait_send()
+            return carry
+
+        lax.fori_loop(1, 16, left, 0)
+        h_copy(g).wait_send()
+        bh_copy(g).wait_send()
     for n in range(5):
         halo_done(n)
     for n in range(4):
@@ -509,6 +558,8 @@
             vmem((4, 32, 8, 128), F32),
             vmem((4, 32, 8, 128), F32),
             vmem((128, 8, 128), F32),
+            vmem((128, 8, 128), F32),
+            vmem((16, 8, 8, 128), F32),
             vmem((16, 8, 8, 128), F32),
             vmem((16, 8, 8, 128), F32),
             vmem((2, 2, 8, 8, 128), F32),
@@ -528,6 +579,7 @@
             vmem((2, 2, 8, 8, 128), F32),
             vmem((16, 8, 8, 128), F32),
             vmem((128, 8, 128), F32),
+            vmem((128, 8, 128), F32),
             vmem((4, 32, 8, 128), F32),
             vmem((4, 32, 8, 128), F32),
             vmem((4, 32, 8, 128), F32),
@@ -545,16 +597,16 @@
             vmem((3, 64, 1), F32),
             dma((6,)),
             dma((4, 2)), dma((4, 2)),
+            dma((PARTS, 4)), dma((PARTS, 4)),
             dma((4,)), dma((4,)),
-            dma((4,)), dma((4,)),
-            dma((4,)), dma((4,)),
-            dma((16,)), dma((16,)),
-            dma, dma,
+            dma((PARTS, 4)), dma((PARTS, 4)),
+            dma((PARTS, 16)), dma((PARTS, 16)),
+            dma((PARTS,)), dma((PARTS,)),
             dma((5, 3)), dma((5, 3)),
-            dma, dma,
-            dma((16,)), dma((16,)),
-            dma((4,)), dma((4,)),
-            dma((4,)), dma((4,)),
+            dma((PARTS,)), dma((PARTS,)),
+            dma((PARTS, 16)), dma((PARTS, 16)),
+            dma((PARTS, 4)), dma((PARTS, 4)),
+            dma((PARTS, 4)), dma((PARTS, 4)),
         ],
         compiler_params=pltpu.CompilerParams(
             collective_id=0, has_side_effects=True, vmem_limit_bytes=60 * 1024 * 1024

time: 131 us -> 120 us (0.916); the launches traced: 130 us -> 120 us
  Pallas kernels: 128 us -> 118 us
    pallas_call x1, Pallas kernels: 128 us -> 118 us  [on_device(): pl.pallas_call(kernel, out_shape=jax.ShapeDtypeStruct((32, 8, 128), F32),...]
where the time goes in v3:
time: 120 us
  Pallas kernels  118 us (98%)
  local copies, waits for them, and re-layouts  1.57 us (1%)
    pallas_call x1, Pallas kernels, on_device(): pl.pallas_call(kernel, out_shape=jax.ShapeDtypeStruct((32, 8, 128), F32),...  118 us

profile of v3, /device:TPU:1, one launch (start us, length us, event | category | flops | bytes accessed | tf_op | source)
XLA Modules:
  0.0 119.9 jit_solution(9696631509730903002)
XLA Ops:
  0.0 118.3 %shard_map.100 = f32[32,8,128]{2,1,0:T(8,128)} custom-call(s32[1,2]{1,0:T(1,128)} %anchor_in.1, s32[1,3]{1,0:T(1,128)} %source_in.1, f32[1,3]{1,0:T(1,128)} %wavelet_in.1, s32[3,1,64]{2,1,0:T(1,128)} %bitcast.2, f32[3,1,64]{2,1,0:T(1,128)} %bitcast.3, f32[32,8,128]{2,1,0:T(8,128)} %courant.1, f32[1,4,128,128]{3,2,1,0:T(8,128)} %wave_before.1, ...), custom_call_target="tpu_custom_call" | custom-call | tf_op jit(solution)/shard_map/pallas_call | solution.py:552
  118.4 1.6 %copy.12 = f32[32,8,128]{2,1,0:T(8,128)} copy(f32[32,8,128]{2,1,0:T(8,128)} %shard_map.100) | data formatting | bytes 262144

commit v4 on v3

--- a/solution.py
+++ b/solution.py
@@ -18,7 +18,7 @@
     anchor_in, source_in, wavelet_in, receivers_in, observed_in, courant, wave_before, wave_now,
     adjoint_after, adjoint_now, out,
     gath, picked, rows_0, rows_1, rowsend, cols_0, cols_1, halfsend, half, twice, speed,
-    pad, before, after_now, after, laps, third, adj, spot, images,
+    pad, ends, sides, before, after_now, after, laps, third, adj, spot, images,
     back_half, back_in, back_send, back_rows_0, back_rows_1, back_pick, back_in_x, back_sum, back_in_y,
     anchors, anchor_own, anchor, source, wavelet, receivers, observed, band, hits, deeps, seens,
     local_sem, field_send, field_recv, y_send, y_recv, a_send, a_recv, x_send, x_recv,
@@ -53,29 +53,6 @@
     def landed(dst, sem):
         pltpu.make_async_copy(dst, dst, sem).wait()
 
-    small = [
-        pltpu.make_async_copy(src, dst, local_sem.at[1 + n])
-        for n, (src, dst) in enumerate(
-            (
-                (anchor_in, anchor), (source_in, source), (wavelet_in, wavelet),
-                (receivers_in, receivers), (observed_in, observed),
-            )
-        )
-    ]
-    for copy in small:
-        copy.start()
-
-    for n in range(5):
-        pad[n, 0:4] = jnp.zeros((4, 80, 128), F32)
-        pad[n, 12:16] = jnp.zeros((4, 80, 128), F32)
-        pad[n, 4:12, 0:8] = jnp.zeros((8, 8, 128), F32)
-        pad[n, 4:12, 72:80] = jnp.zeros((8, 8, 128), F32)
-    for copy in small:
-        copy.wait()
-    ox, oy = anchor[0, 0], anchor[0, 1]
-    anchor_own[...] = jnp.full((8, 128), ox, I32)
-    anchors[x] = jnp.full((8, 128), ox, I32)
-
     barrier = pltpu.get_barrier_semaphore()
     for d in range(1, 4):
         pl.semaphore_signal(barrier, 1, device_id=at_x((x + d) % 4), device_id_type=MESH)
@@ -84,6 +61,25 @@
         pl.semaphore_signal(barrier, 1, device_id=at_k((k + d) % 16), device_id_type=MESH)
     pl.semaphore_signal(barrier, 1, device_id=partner, device_id_type=MESH)
     pl.semaphore_signal(barrier, 1, device_id=diagonal, device_id_type=MESH)
+    small = [
+        pltpu.make_async_copy(src, dst, local_sem.at[1 + n])
+        for n, (src, dst) in enumerate(
+            (
+                (anchor_in, anchor), (source_in, source), (wavelet_in, wavelet),
+                (receivers_in, receivers), (observed_in, observed),
+            )
+        )
+    ]
+    for copy in small:
+        copy.start()
+
+    for copy in small:
+        copy.wait()
+    ox, oy = anchor[0, 0], anchor[0, 1]
+    anchor_own[...] = jnp.full((8, 128), ox, I32)
+    anchors[x] = jnp.full((8, 128), ox, I32)
+
+
     pl.semaphore_wait(barrier, 23)
 
     def part(g):
@@ -145,6 +141,30 @@
         src, dst = field_parts(n)
         for core in range(2):
             landed(dst(core), field_recv.at[n, core])
+
+    for n in range(5):
+        pad[n, 0:4] = jnp.zeros((4, 80, 128), F32)
+        pad[n, 12:16] = jnp.zeros((4, 80, 128), F32)
+        pad[n, 4:12, 0:8] = jnp.zeros((8, 8, 128), F32)
+        pad[n, 4:12, 72:80] = jnp.zeros((8, 8, 128), F32)
+        sides[n, :, 8:16] = jnp.zeros((8, 8, 128), F32)
+
+    @pl.when(yh == 0)
+    def _():
+        for n in range(5):
+            sides[n, :, 4:8] = jnp.zeros((8, 4, 128), F32)
+
+    @pl.when(yh == 1)
+    def _():
+        for n in range(5):
+            sides[n, :, 16:20] = jnp.zeros((8, 4, 128), F32)
+
+    for side, first_or_last in ((0, 0), (1, 15)):
+
+        @pl.when(k == first_or_last)
+        def _():
+            for n in range(5):
+                ends[n, side] = jnp.zeros((4, 64, 128), F32)
 
     square = lax.broadcasted_iota(I32, (64, 64), 0) == lax.broadcasted_iota(I32, (64, 64), 1)
 
@@ -193,60 +213,110 @@
             precision=HIGH, preferred_element_type=F32,
         ).reshape(8, 64, 128)
 
-    def halo_parts(n):
-        up = push(
-            pad.at[n, pl.ds(4, 4), pl.ds(8, 64)], pad.at[n, pl.ds(12, 4), pl.ds(8, 64)],
-            halo_send.at[n, 0], halo_recv.at[n, 0], at_k((k + 15) % 16),
-        )
-        down = push(
-            pad.at[n, pl.ds(8, 4), pl.ds(8, 64)], pad.at[n, pl.ds(0, 4), pl.ds(8, 64)],
-            halo_send.at[n, 1], halo_recv.at[n, 1], at_k((k + 1) % 16),
-        )
-        side = push(
-            pad.at[n, pl.ds(4, 8), pl.ds(pl.multiple_of(64 - 56 * yh, 8), 8)],
-            pad.at[n, pl.ds(4, 8), pl.ds(pl.multiple_of(72 * yh, 8), 8)],
+    def end_copy(n, way):
+        return push(
+            pad.at[n, pl.ds(4 + 4 * way, 4), pl.ds(8, 64)], ends.at[n, 1 - way],
+            halo_send.at[n, way], halo_recv.at[n, way], at_k((k + 15 + 2 * way) % 16),
+        )
+
+    def side_copy(n, half_of):
+        return push(
+            pad.at[n, pl.ds(4, 8), pl.ds(68 - 60 * half_of, 4)],
+            sides.at[n, :, pl.ds(4 + 12 * half_of, 4)],
             halo_send.at[n, 2], halo_recv.at[n, 2], partner,
         )
-        return up, down, side
+
+    def end_there(way):
+        return k > 0 if way == 0 else k < 15
+
+    def end_start(n, way):
+        @pl.when(end_there(way))
+        def _():
+            end_copy(n, way).start()
+
+    def side_start(n):
+        for half_of in range(2):
+
+            @pl.when(yh == half_of)
+            def _():
+                side_copy(n, half_of).start()
 
     def halo_start(n):
-        up, down, side = halo_parts(n)
-
-        @pl.when(k > 0)
+        side_start(n)
+        for way in range(2):
+            end_start(n, way)
+
+    def halo_wait(n):
+        for way in range(2):
+
+            @pl.when(end_there(1 - way))
+            def _():
+                landed(ends.at[n, 1 - way], halo_recv.at[n, way])
+
+        for half_of in range(2):
+
+            @pl.when(yh != half_of)
+            def _():
+                landed(sides.at[n, :, pl.ds(4 + 12 * half_of, 4)], halo_recv.at[n, 2])
+
+    def halo_done(n):
+        for way in range(2):
+
+            @pl.when(end_there(way))
+            def _():
+                end_copy(n, way).wait_send()
+
+        for half_of in range(2):
+
+            @pl.when(yh == half_of)
+            def _():
+                side_copy(n, half_of).wait_send()
+
+    def close(n, lap, new, weight, send):
+        def add(row, at, wide, extra):
+            if lap is not None:
+                lap[row, pl.ds(at, wide)] = lap[row, pl.ds(at, wide)] + extra
+            below, right = (4, 8) if send else (0, 0)
+            place = pl.ds(pl.multiple_of(right + at, 8), wide)
+            new[below + row, place] = new[below + row, place] + weight[row, pl.ds(at, wide)] * extra
+
+        def from_end(way, i, at, wide):
+            total = None
+            for d in range(i + 1, 5):
+                row = 4 + i - d if way == 0 else d - i - 1
+                term = COEF[d] * ends[n, way, row, pl.ds(at, wide)]
+                total = term if total is None else total + term
+            return total
+
+        beside = None
+        for d in range(1, 5):
+            term = COEF[d] * (sides[n, :, 8 - d : 16 - d] + sides[n, :, 8 + d : 16 + d])
+            beside = term if beside is None else beside + term
+        edge = pl.multiple_of(56 - 56 * yh, 8)
+        rest = pl.multiple_of(8 * yh, 8)
+        for way in range(2):
+            for i in range(4):
+                row = i if way == 0 else 7 - i
+                add(row, edge, 8, beside[row] + from_end(way, i, edge, 8))
+        if send:
+            side_start(n + 1)
+
+        def rows_of(way):
+            for i in range(4):
+                row = i if way == 0 else 7 - i
+                add(row, rest, 56, from_end(way, i, rest, 56))
+            if send:
+                end_start(n + 1, way)
+
+        @pl.when(c == 0)
         def _():
-            up.start()
-
-        @pl.when(k < 15)
+            rows_of(0)
+            rows_of(1)
+
+        @pl.when(c == 1)
         def _():
-            down.start()
-
-        side.start()
-
-    def halo_wait(n):
-        @pl.when(k > 0)
-        def _():
-            landed(pad.at[n, pl.ds(0, 4), pl.ds(8, 64)], halo_recv.at[n, 1])
-
-        @pl.when(k < 15)
-        def _():
-            landed(pad.at[n, pl.ds(12, 4), pl.ds(8, 64)], halo_recv.at[n, 0])
-
-        landed(
-            pad.at[n, pl.ds(4, 8), pl.ds(pl.multiple_of(72 - 72 * yh, 8), 8)], halo_recv.at[n, 2]
-        )
-
-    def halo_done(n):
-        up, down, side = halo_parts(n)
-
-        @pl.when(k > 0)
-        def _():
-            up.wait_send()
-
-        @pl.when(k < 15)
-        def _():
-            down.wait_send()
-
-        side.wait_send()
+            rows_of(1)
+            rows_of(0)
 
     def laplace(n):
         total = jnp.dot(
@@ -353,8 +423,12 @@
             halo_start(0)
     field_start(2)
     field_start(3)
+    laps[0] = laplace(0)
+    field_wait(1)
+    pad[1, 4:12, 8:72] = 2.0 * pad[0, 4:12, 8:72] - before[...] + wavelet[0, 0] * spot[...]
+    third[...] = jnp.zeros((8, 64, 128), F32)
     halo_wait(0)
-    laps[0] = laplace(0)
+    close(0, laps.at[0], third, spot, False)
     for g in range(PARTS):
         landed(half.at[1 - yh, :, :, :, part(g), :], h_recv.at[g])
     for e in range(2):
@@ -366,49 +440,41 @@
     for r in range(8):
         speed[r] = twice[r, pl.ds(turn, 64)]
 
-    field_wait(1)
-    now = pad[0, 4:12, 8:72]
-    new = 2.0 * now - before[...] + speed[...] * laps[0] + wavelet[0, 0] * spot[...]
-    pad[1, 4:12, 8:72] = new
+    pad[1, 4:12, 8:72] = pad[1, 4:12, 8:72] + speed[...] * laps[0]
     halo_start(1)
-    residual0 = record(new, 0)
+    laps[1] = laplace(1)
+    pad[2, 4:12, 8:72] = (
+        2.0 * pad[1, 4:12, 8:72] - pad[0, 4:12, 8:72] + wavelet[0, 1] * spot[...]
+        + speed[...] * laps[1]
+    )
+    residual0 = record(pad[1, 4:12, 8:72], 0)
     halo_wait(1)
-    lap = laplace(1)
-    laps[1] = lap
-    new = (
-        2.0 * pad[1, 4:12, 8:72] - pad[0, 4:12, 8:72] + speed[...] * lap
-        + wavelet[0, 1] * spot[...]
+    close(1, laps.at[1], pad.at[2], speed, True)
+    laps[2] = laplace(2)
+    third[...] = (
+        2.0 * pad[2, 4:12, 8:72] - pad[1, 4:12, 8:72] + wavelet[0, 2] * spot[...]
+        + speed[...] * laps[2]
     )
-    pad[2, 4:12, 8:72] = new
-    halo_start(2)
-    residual1 = record(new, 1)
+    residual1 = record(pad[2, 4:12, 8:72], 1)
     halo_wait(2)
-    lap = laplace(2)
-    laps[2] = lap
-    new = (
-        2.0 * pad[2, 4:12, 8:72] - pad[1, 4:12, 8:72] + speed[...] * lap
-        + wavelet[0, 2] * spot[...]
-    )
-    third[...] = new
+    close(2, laps.at[2], third, speed, False)
     residual2 = record(third[...], 2)
 
     field_wait(2)
     adj[0] = after_now[...] + inject(residual2)
     pad[3, 4:12, 8:72] = speed[...] * adj[0]
     halo_start(3)
+    field_wait(3)
+    adj[1] = 2.0 * adj[0] - after[...] + inject(residual1) + laplace(3)
+    pad[4, 4:12, 8:72] = speed[...] * adj[1]
     images[:, 0:64] = adj[0] * laps[2]
-    field_wait(3)
-    adj[1] = 2.0 * adj[0] - after[...] + inject(residual1)
     halo_wait(3)
-    adj[1] = adj[1] + laplace(3)
-    pad[4, 4:12, 8:72] = speed[...] * adj[1]
-    halo_start(4)
-    images[:, 0:64] = images[:, 0:64] + adj[1] * laps[1]
-    third[...] = 2.0 * adj[1] - adj[0] + inject(residual0)
+    close(3, adj.at[1], pad.at[4], speed, True)
+    third[...] = 2.0 * adj[1] - adj[0] + inject(residual0) + laplace(4)
+    images[:, 0:64] = images[:, 0:64] + adj[1] * laps[1] + third[...] * laps[0]
     halo_wait(4)
-    image = images[:, 0:64] + (third[...] + laplace(4)) * laps[0]
-    images[:, 0:64] = image
-    images[:, 64:128] = image
+    close(4, None, images, laps.at[0], False)
+    images[:, 64:128] = images[:, 0:64]
 
     for r in range(8):
         line = images[r, pl.ds(64 - turn, 64)]
@@ -567,6 +633,8 @@
             vmem((8, 128, 128), F32),
             vmem((8, 64, 128), F32),
             vmem((5, 16, 80, 128), F32),
+            vmem((5, 2, 4, 64, 128), F32),
+            vmem((5, 8, 24, 128), F32),
             vmem((8, 64, 128), F32),
             vmem((8, 64, 128), F32),
             vmem((8, 64, 128), F32),

time: 120 us -> 114 us (0.950)
  Pallas kernels: 118 us -> 112 us
    pallas_call x1, Pallas kernels: 118 us -> 112 us  [on_device(): pl.pallas_call(kernel, out_shape=jax.ShapeDtypeStruct((32, 8, 128), F32),...]
where the time goes in v4:
time: 114 us
  Pallas kernels  112 us (98%)
  local copies, waits for them, and re-layouts  1.57 us (1%)
    pallas_call x1, Pallas kernels, on_device(): pl.pallas_call(kernel, out_shape=jax.ShapeDtypeStruct((32, 8, 128), F32),...  112 us

profile of v4, /device:TPU:1, one launch (start us, length us, event | category | flops | bytes accessed | tf_op | source)
XLA Modules:
  0.0 113.7 jit_solution(8995802327081789491)
XLA Ops:
  0.0 112.1 %shard_map.100 = f32[32,8,128]{2,1,0:T(8,128)} custom-call(s32[1,2]{1,0:T(1,128)} %anchor_in.1, s32[1,3]{1,0:T(1,128)} %source_in.1, f32[1,3]{1,0:T(1,128)} %wavelet_in.1, s32[3,1,64]{2,1,0:T(1,128)} %bitcast.2, f32[3,1,64]{2,1,0:T(1,128)} %bitcast.3, f32[32,8,128]{2,1,0:T(8,128)} %courant.1, f32[1,4,128,128]{3,2,1,0:T(8,128)} %wave_before.1, ...), custom_call_target="tpu_custom_call" | custom-call | tf_op jit(solution)/shard_map/pallas_call | solution.py:618
  112.1 1.6 %copy.12 = f32[32,8,128]{2,1,0:T(8,128)} copy(f32[32,8,128]{2,1,0:T(8,128)} %shard_map.100) | data formatting | bytes 262144

commit v5 on v4

--- a/solution.py
+++ b/solution.py
@@ -23,7 +23,7 @@
     anchors, anchor_own, anchor, source, wavelet, receivers, observed, band, hits, deeps, seens,
     local_sem, field_send, field_recv, y_send, y_recv, a_send, a_recv, x_send, x_recv,
     s_send, s_recv, h_send, h_recv, halo_send, halo_recv,
-    bh_send, bh_recv, bs_send, bs_recv, bx_send, bx_recv, by_send, by_recv,
+    bh_send, bh_recv, bs_send, bs_recv, bx_send, bx_recv, by_send, by_recv, relay_send,
 ):
     rows, cols, back_rows = (rows_0, rows_1), (cols_0, cols_1), (back_rows_0, back_rows_1)
     shot = lax.axis_index("shot")
@@ -94,6 +94,17 @@
     own_model = pltpu.make_async_copy(courant, gath.at[yl], local_sem.at[0])
     own_model.start()
 
+    def y_direct(d):
+        if d == 2:
+            return yl >= 0
+        return yl != (0 if d == 3 else 3)
+
+    inner = jnp.logical_and(yl > 0, yl < 3)
+
+    def y_relay(g):
+        slot = gath.at[(yl + 2) % 4, :, part(g), :]
+        return push(slot, slot, relay_send.at[g], y_recv.at[g, 2 * yl - 1], at_y(3 * (yl - 1)))
+
     def a_copy(d):
         return push(anchor_own, anchors.at[x], a_send.at[d], a_recv.at[d], at_x((x + d) % 4))
 
@@ -101,7 +112,10 @@
         a_copy(d).start()
     for g in range(PARTS):
         for d in (2, 1, 3):
-            y_copy(g, d).start()
+
+            @pl.when(y_direct(d))
+            def _():
+                y_copy(g, d).start()
 
     def field_parts(n):
         src = (wave_now, wave_before, adjoint_now, adjoint_after)[n]
@@ -346,7 +360,13 @@
         )
 
     for g in range(PARTS):
-        for d in (1, 3, 2):
+        landed(gath.at[(yl + 2) % 4, :, part(g), :], y_recv.at[g, 2])
+
+        @pl.when(inner)
+        def _():
+            y_relay(g).start()
+
+        for d in (1, 3):
             landed(gath.at[(yl + 4 - d) % 4, :, part(g), :], y_recv.at[g, d])
         for d in (2, 1, 3, 0):
             which = super_of((x + d) % 4, g)
@@ -586,7 +606,11 @@
         a_copy(d).wait_send()
     for g in range(PARTS):
         for d in (1, 2, 3):
-            y_copy(g, d).wait_send()
+
+            @pl.when(y_direct(d))
+            def _():
+                y_copy(g, d).wait_send()
+
             x_copy(g, d).wait_send()
             bx_copy(g, d).wait_send()
             by_copy(g, d).wait_send()
@@ -599,6 +623,10 @@
         lax.fori_loop(1, 16, left, 0)
         h_copy(g).wait_send()
         bh_copy(g).wait_send()
+
+        @pl.when(inner)
+        def _():
+            y_relay(g).wait_send()
     for n in range(5):
         halo_done(n)
     for n in range(4):
@@ -675,6 +703,7 @@
             dma((PARTS, 16)), dma((PARTS, 16)),
             dma((PARTS, 4)), dma((PARTS, 4)),
             dma((PARTS, 4)), dma((PARTS, 4)),
+            dma((PARTS,)),
         ],
         compiler_params=pltpu.CompilerParams(
             collective_id=0, has_side_effects=True, vmem_limit_bytes=60 * 1024 * 1024

time: 114 us -> 113 us (level)
  no operation moved by 1% of the time
where the time goes in v5:
time: 113 us
  Pallas kernels  111 us (98%)
  local copies, waits for them, and re-layouts  1.57 us (1%)
    pallas_call x1, Pallas kernels, on_device(): pl.pallas_call(kernel, out_shape=jax.ShapeDtypeStruct((32, 8, 128), F32),...  111 us

profile of v5, /device:TPU:1, one launch (start us, length us, event | category | flops | bytes accessed | tf_op | source)
XLA Modules:
  0.0 113.0 jit_solution(9736232571477873026)
XLA Ops:
  0.0 111.5 %shard_map.100 = f32[32,8,128]{2,1,0:T(8,128)} custom-call(s32[1,2]{1,0:T(1,128)} %anchor_in.1, s32[1,3]{1,0:T(1,128)} %source_in.1, f32[1,3]{1,0:T(1,128)} %wavelet_in.1, s32[3,1,64]{2,1,0:T(1,128)} %bitcast.2, f32[3,1,64]{2,1,0:T(1,128)} %bitcast.3, f32[32,8,128]{2,1,0:T(8,128)} %courant.1, f32[1,4,128,128]{3,2,1,0:T(8,128)} %wave_before.1, ...), custom_call_target="tpu_custom_call" | custom-call | tf_op jit(solution)/shard_map/pallas_call | solution.py:646
  111.5 1.6 %copy.12 = f32[32,8,128]{2,1,0:T(8,128)} copy(f32[32,8,128]{2,1,0:T(8,128)} %shard_map.100) | data formatting | bytes 262144

commit v6 on v5

--- a/solution.py
+++ b/solution.py
@@ -438,9 +438,8 @@
         for e in range(2):
             for core in range(2):
                 half[yh, e, core, :, part(g), :] = columns(yh, e, core, g)
-        if g == 0:
-            field_wait(0)
-            halo_start(0)
+    field_wait(0)
+    halo_start(0)
     field_start(2)
     field_start(3)
     laps[0] = laplace(0)

time: 113 us -> 112 us (level)
  no operation moved by 1% of the time
where the time goes in v6:
time: 112 us
  Pallas kernels  111 us (99%)
  local copies, waits for them, and re-layouts  1.57 us (1%)
    pallas_call x1, Pallas kernels, on_device(): pl.pallas_call(kernel, out_shape=jax.ShapeDtypeStruct((32, 8, 128), F32),...  111 us

profile of v6, /device:TPU:1, one launch (start us, length us, event | category | flops | bytes accessed | tf_op | source)
XLA Modules:
  0.0 112.2 jit_solution(12587774270961652506)
XLA Ops:
  0.0 110.6 %shard_map.100 = f32[32,8,128]{2,1,0:T(8,128)} custom-call(s32[1,2]{1,0:T(1,128)} %anchor_in.1, s32[1,3]{1,0:T(1,128)} %source_in.1, f32[1,3]{1,0:T(1,128)} %wavelet_in.1, s32[3,1,64]{2,1,0:T(1,128)} %bitcast.2, f32[3,1,64]{2,1,0:T(1,128)} %bitcast.3, f32[32,8,128]{2,1,0:T(8,128)} %courant.1, f32[1,4,128,128]{3,2,1,0:T(8,128)} %wave_before.1, ...), custom_call_target="tpu_custom_call" | custom-call | tf_op jit(solution)/shard_map/pallas_call | solution.py:645
  110.6 1.6 %copy.12 = f32[32,8,128]{2,1,0:T(8,128)} copy(f32[32,8,128]{2,1,0:T(8,128)} %shard_map.100) | data formatting | bytes 262144
